TPU v7x, 512 devices: a whole 4x4x16 slice. The times are simulated.
512 devices in a mesh: vocab: 128 (over y, z, core), width: 4 (over x).
Axes of the slice: x: 4, y: 4, z: 16, core: 2. Of those that a mesh axis runs over, the one named last changes fastest.
Arguments:
- hidden: bfloat16 [256, 4608], P(None, 'width'), may hold values from -6 to 6
- head_weight: bfloat16 [262144, 4608], P('vocab', 'width'), as said below
- targets: int32 [256], replicated, may hold values from 0 to 262143
- token_scale: float32 [256], replicated, may hold values from 8 to 64
Outputs:
- hidden_grad: bfloat16 [256, 4608], P('vocab', 'width')
Inputs may be any that keep to these rules, and one draw needn't show every extreme that they name: Each row of head_weight is independent noise of its own scale.
All inputs are finite; a program needn't handle non-finite values.
Results may differ from a plain program's by a relative error of at most 0.0046.
Values may be sent and summed in bfloat16 or wider, within the bound.
No kernel may reach another device: no remote copies, remote signals or barrier semaphores. Data moves between devices by JAX's collectives and lax.ppermute only.
A program may use at most 64 MiB of HBM per device.

v0:
```python
import jax
import jax.numpy as jnp
from jax import lax
from jax.sharding import PartitionSpec as P

logit_cap = 30.0
zloss_weight = 0.001


def grad_block(partial_raw, targets, token_scale, col_offset, total):
    tangent = jnp.tanh(partial_raw / logit_cap)
    exp_terms = jnp.exp(logit_cap * tangent)
    log_total = jnp.log(total)
    weighting = token_scale * (1.0 + 2.0 * zloss_weight * log_total)
    columns = col_offset + lax.broadcasted_iota(jnp.int32, partial_raw.shape, 1)
    matches = (targets[:, None] == columns).astype(jnp.float32)
    capped_grad = weighting[:, None] * exp_terms / total[:, None] - token_scale[:, None] * matches
    return (capped_grad * (1.0 - tangent * tangent)).astype(jnp.bfloat16)


def on_device(hidden, head_weight, targets, token_scale):
    local_vocab = head_weight.shape[0]
    vocab_offset = lax.axis_index("vocab") * local_vocab
    partial_logits = lax.dot_general(
        hidden, head_weight, (((1,), (1,)), ((), ())), preferred_element_type=jnp.float32
    )
    logits = lax.psum(partial_logits, "width")
    row_total = jnp.sum(jnp.exp(logit_cap * jnp.tanh(logits / logit_cap)), axis=1)
    total = lax.psum(row_total, "vocab")
    raw_grad = grad_block(logits, targets, token_scale, vocab_offset, total)
    summed = lax.psum_scatter(
        jnp.dot(raw_grad, head_weight, preferred_element_type=jnp.float32),
        "vocab",
        scatter_dimension=0,
        tiled=True,
    )
    return summed.astype(jnp.bfloat16)


def solution(mesh):
    placed = (P(None, "width"), P("vocab", "width"), P(), P())
    return jax.shard_map(
        on_device, mesh=mesh, in_specs=placed, out_specs=P("vocab", "width"), check_vma=False
    )
```

profile of v0, /device:TPU:6, one launch (start us, length us, event | category | flops | bytes accessed | tf_op | source)
XLA Modules:
  0.0 860.3 jit_solution(7007714849184166746)
XLA Ops:
  6.5 0.0 copy-start
  6.5 0.0 all-reduce.4.cloned.1.call-start
  6.5 1.1 copy-done
  7.6 5.2 fusion.15
  12.8 0.0 copy-start.2
  12.8 0.0 copy-start.3
  12.8 0.0 all-reduce.4.cloned.1.call-update
  12.8 1.3 dynamic-slice
  14.8 74.9 %all-reduce.4.cloned.1.call-done = f32[256,2048]{1,0:T(8,128)} async-done(((f32[256,2048]{1,0:T(8,128)}), f32[256,2048]{1,0:T(8,128)}) %all-reduce.4.cloned.1.call-update) | async-done | bytes 2097168 | tf_op jit(solution)/shard_map/psum | solution.py:27
  89.6 0.0 copy-start.1
  89.6 2.4 fusion
  92.0 252.5 %psum.15 = f32[256]{0:T(256)S(1)} all-reduce(f32[256]{0:T(256)S(1)} %fusion), channel_id=1, replica_groups=mesh['vocab'=128,'width'=4] {'vocab'}, use_global_device_ids=true, to_apply=%region_2.0 | all-reduce | flops 256 | bytes 2048 | tf_op jit(solution)/shard_map/psum | solution.py:29
  344.4 0.0 copy-done.2
  344.4 0.0 copy-done.3
  344.5 0.0 copy-done.1
  344.5 5.4 fusion.1
  349.9 503.0 %all-reduce.5 = bf16[256,1152]{1,0:T(8,128)(2,1)S(1)} all-reduce(f32[256,1152]{1,0:T(8,128)} %fusion.1), channel_id=2, replica_groups=mesh['vocab'=128,'width'=4] {'vocab'}, use_global_device_ids=true, to_apply=%region_3.0.clone | all-reduce | flops 294912 | bytes 1769472
  852.9 0.6 dynamic-slice_convert_fusion
  (2 shorter events, 0.0 us)
Async XLA Ops:
  6.5 1.1 copy-start
  6.5 83.1 %all-reduce.4.cloned.1.call-start = ((), (), s32[]{:S(2)}) async-start(), calls=%async_computation | async-start | bytes 4194304 | tf_op jit(solution)/shard_map/psum | solution.py:27
  12.8 331.7 %copy-start.2 = (f32[256]{0:T(256)S(1)}, f32[256]{0:T(256)}, u32[]{:S(2)}) copy-start(f32[256]{0:T(256)} %param.7) | copy-start | bytes 3076
  12.8 331.7 %copy-start.3 = (s32[256]{0:T(256)S(1)}, s32[256]{0:T(256)}, u32[]{:S(2)}) copy-start(s32[256]{0:T(256)} %param.6) | copy-start | bytes 3076
  89.6 254.8 %copy-start.1 = (f32[256,2048]{1,0:T(8,128)S(1)}, f32[256,2048]{1,0:T(8,128)}, u32[]{:S(2)}) copy-start(f32[256,2048]{1,0:T(8,128)} %all-reduce.4.cloned.1.call-done) | copy-start | bytes 6291460
Sparse Core Ops, SparseCore 0:
  12.9 76.6 all-reduce.3
where the time goes:
time: 861 us; the launch traced here: 860 us
  blocking collectives  755 us (88%)
  waiting for transfers between devices  74.9 us (9%)
  between operations  14.1 us (2%)
  matrix products  10.6 us (1%)
    unnamed x1, blocking collectives  503 us
    psum x1, blocking collectives, on_device(): total = lax.psum(row_total, 'vocab')  252 us
    psum x1, waiting for transfers between devices, on_device(): logits = lax.psum(partial_logits, 'width')  74.9 us
  transfers between devices with their start and end apart: 1, of which 1 were waited for; matrix products, arithmetic and copies ran while one was open for 0% of the time, Pallas kernels for 0%

commit v1 on v0

v1 whole, which is shorter than its diff:
```python
import functools
import jax
import jax.numpy as jnp
from jax import lax
from jax.experimental import pallas as pl
from jax.experimental.pallas import tpu as pltpu
from jax.sharding import Mesh, PartitionSpec as P

logit_cap = 30.0
zloss_weight = 0.001

f32, bf16, i16, i32 = jnp.float32, jnp.bfloat16, jnp.int16, jnp.int32

SIDE = 16
LANES = 128
TOP = 32767.0


def exponent_of(largest):
    return jnp.floor(jnp.log2(jnp.maximum(largest, 1e-30))) - 14.0


def code(values, exponent):
    scaled = jnp.floor(values * jnp.exp2(-exponent) + 0.5)
    return jnp.clip(scaled, -TOP, TOP).astype(i32).astype(i16)


def to_f32(codes):
    return codes.astype(i32).astype(f32)


def token_order(sizes, tokens):
    ny, nz, nc = sizes
    pair = tokens // (ny * nz * nc)
    place = lax.broadcasted_iota(i32, (tokens, tokens), 0)
    token = lax.broadcasted_iota(i32, (tokens, tokens), 1)
    core = place // (ny * nz * pair)
    yz = (place // pair) % (ny * nz)
    r = place % pair
    return token == (yz * nc + core) * pair + r


def column_of(mask, row):
    return jnp.sum(jnp.where(mask, row, 0.0), axis=1, keepdims=True)


def eye(n):
    return lax.broadcasted_iota(i32, (n, n), 0) == lax.broadcasted_iota(i32, (n, n), 1)


def logits_kernel(sizes, hidden_ref, weight_ref, out_ref, ordered_ref):
    tokens = hidden_ref.shape[0]

    @pl.when(pl.program_id(0) == 0)
    def _():
        order = jnp.where(token_order(sizes, tokens), 1.0, 0.0).astype(bf16)
        ordered_ref[...] = jnp.dot(
            order, hidden_ref[...], preferred_element_type=f32
        ).astype(bf16)

    partial = lax.dot_general(
        ordered_ref[...], weight_ref[...], (((1,), (1,)), ((), ())), preferred_element_type=f32
    )
    exponent = exponent_of(jnp.max(jnp.abs(partial), axis=0, keepdims=True))
    out_ref[0, 0:tokens, :] = code(partial, exponent)
    out_ref[0, tokens:, :] = jnp.broadcast_to(
        exponent, (SIDE, exponent.shape[1])
    ).astype(i32).astype(i16)


def exp_kernel(sizes, codes_ref, targets_ref, out_ref):
    parts, rows, columns = codes_ref.shape
    tokens = rows - SIDE
    raw = None
    for part in range(parts):
        exponent = to_f32(codes_ref[part, tokens:, :])[0:1]
        term = to_f32(codes_ref[part, 0:tokens, :]) * jnp.exp2(exponent)
        raw = term if raw is None else raw + term
    tangent = jnp.tanh(raw / logit_cap)
    exp_terms = jnp.exp(logit_cap * tangent)
    slope = 1.0 - tangent * tangent
    grads = (exp_terms * slope).astype(bf16)
    sums = jnp.sum(exp_terms, axis=1, keepdims=True)
    targets = column_of(token_order(sizes, tokens), targets_ref[...].astype(f32))
    places = lax.broadcasted_iota(i32, raw.shape, 1).astype(f32)
    at_target = jnp.sum(jnp.where(targets == places, slope, 0.0), axis=1, keepdims=True)
    diagonal = eye(tokens)
    sum_row = jnp.sum(jnp.where(diagonal, sums, 0.0), axis=0, keepdims=True)
    target_row = jnp.sum(jnp.where(diagonal, at_target, 0.0), axis=0, keepdims=True)
    which = lax.broadcasted_iota(i32, (SIDE, tokens), 0)
    side = jnp.where(which == 0, sum_row, jnp.where(which == 1, target_row, 0.0))
    high = side.astype(bf16)
    low = (side - high.astype(f32)).astype(bf16)
    pieces = [high, low]
    if columns > 2 * tokens:
        pieces.append(jnp.zeros((SIDE, columns - 2 * tokens), bf16))
    side = jnp.concatenate(pieces, axis=1)
    for part in range(parts):
        out_ref[part, 0:tokens, :] = grads
        out_ref[part, tokens:, :] = side


def hidden_kernel(sizes, grads_ref, weight_ref, targets_ref, out_ref, side_ref):
    step = pl.program_id(0)
    nc = sizes[2]
    _, rows, columns = grads_ref.shape
    tokens = rows - SIDE
    width = weight_ref.shape[1]
    own = tokens // nc
    targets = column_of(token_order(sizes, tokens), targets_ref[...].astype(f32))
    places = (lax.broadcasted_iota(i32, (tokens, columns), 1) + step * columns).astype(f32)
    at_target = jnp.where(targets == places, 1.0, 0.0).astype(bf16)
    weight = weight_ref[...]
    soft = jnp.dot(grads_ref[0, 0:tokens, :], weight, preferred_element_type=f32)
    hard = jnp.dot(at_target, weight, preferred_element_type=f32)
    side = grads_ref[0, tokens:, :].astype(f32)
    side = side[:, 0:tokens] + side[:, tokens : 2 * tokens]

    @pl.when(step == 0)
    def _():
        side_ref[...] = side
        for c in range(nc):
            out_ref[c, :, 0:width] = soft[c * own : (c + 1) * own]
            out_ref[c, :, width : 2 * width] = hard[c * own : (c + 1) * own]

    @pl.when(step > 0)
    def _():
        side_ref[...] += side
        for c in range(nc):
            out_ref[c, :, 0:width] += soft[c * own : (c + 1) * own]
            out_ref[c, :, width : 2 * width] += hard[c * own : (c + 1) * own]

    @pl.when(step == pl.num_programs(0) - 1)
    def _():
        diagonal = eye(tokens)
        sums = column_of(diagonal, side_ref[0:1, :])
        slope = column_of(diagonal, side_ref[1:2, :])
        for c in range(nc):
            part = slice(c * own, (c + 1) * own)
            out_ref[c, :, width : 2 * width] *= slope[part]
            out_ref[c, :, 2 * width :] = jnp.broadcast_to(sums[part], (own, LANES))


def coded_rows(soft, hard, total):
    rows = soft.shape[0]
    soft_exp = exponent_of(jnp.max(jnp.abs(soft), axis=1, keepdims=True))
    hard_exp = exponent_of(jnp.max(jnp.abs(hard), axis=1, keepdims=True))
    total_exp = jnp.floor(jnp.log2(jnp.maximum(total, 1e-30))) - 24.0
    scaled = total * jnp.exp2(-total_exp)
    high = jnp.floor(scaled * (1.0 / 4096.0))
    low = scaled - high * 4096.0
    lane = lax.broadcasted_iota(i32, (rows, LANES), 1)
    side = jnp.where(lane == 0, soft_exp, 0.0)
    for at, value in enumerate((hard_exp, total_exp, high, low), 1):
        side = jnp.where(lane == at, value, side)
    side = side.astype(i32).astype(i16)
    return code(soft, soft_exp), code(hard, hard_exp), side


def decoded(codes, width):
    side = to_f32(codes[:, 2 * width :])
    soft = to_f32(codes[:, 0:width]) * jnp.exp2(side[:, 0:1])
    hard = to_f32(codes[:, width : 2 * width]) * jnp.exp2(side[:, 1:2])
    total = (side[:, 3:4] * 4096.0 + side[:, 4:5]) * jnp.exp2(side[:, 2:3])
    return soft, hard, total


def store_rows(out_ref, soft, hard, total, width):
    parts, rows, _ = out_ref.shape
    coded = coded_rows(soft, hard, total)
    at = 0
    for piece in coded:
        for part in range(parts):
            out_ref[part, :, at : at + piece.shape[1]] = piece[part * rows : (part + 1) * rows]
        at += piece.shape[1]


def cores_kernel(width, in_ref, out_ref):
    total = in_ref[0]
    for c in range(1, in_ref.shape[0]):
        total = total + in_ref[c]
    soft, hard = total[:, 0:width], total[:, width : 2 * width]
    store_rows(out_ref, soft, hard, total[:, 2 * width : 2 * width + 1], width)


def y_kernel(width, in_ref, out_ref):
    terms = [decoded(in_ref[part], width) for part in range(in_ref.shape[0])]
    soft, hard, total = (functools.reduce(jnp.add, t) for t in zip(*terms))
    store_rows(out_ref, soft, hard, total, width)


def whole(shape):
    return pl.BlockSpec(shape, lambda *_: (0,) * len(shape))


def params():
    return pltpu.CompilerParams(vmem_limit_bytes=40 * 1024 * 1024)


def on_device(sizes, hidden, head_weight, targets, token_scale):
    ny, nz, nc = sizes
    nw = lax.axis_size("w")
    tokens, width = hidden.shape
    vocab = head_weight.shape[0]
    columns = vocab // nw
    rows = tokens + SIDE
    pair = tokens // (ny * nz * nc)
    lanes = 2 * width + LANES
    device = (lax.axis_index("y") * nz + lax.axis_index("z")) * nc + lax.axis_index("c")
    shard_targets = (targets - device * vocab).reshape(1, tokens)
    block_targets = shard_targets - lax.axis_index("w") * columns

    codes = pl.pallas_call(
        functools.partial(logits_kernel, sizes),
        grid=(nw,),
        in_specs=[whole((tokens, width)), pl.BlockSpec((columns, width), lambda j: (j, 0))],
        out_specs=pl.BlockSpec((1, rows, columns), lambda j: (j, 0, 0)),
        out_shape=jax.ShapeDtypeStruct((nw, rows, columns), i16),
        scratch_shapes=[pltpu.VMEM((tokens, width), bf16)],
        compiler_params=params(),
        name="logits",
    )(hidden, head_weight)
    codes = lax.all_to_all(codes, "w", 0, 0, tiled=True)
    grads = pl.pallas_call(
        functools.partial(exp_kernel, sizes),
        out_shape=jax.ShapeDtypeStruct((nw, rows, columns), bf16),
        compiler_params=params(),
        name="exponentials",
    )(codes, block_targets)
    grads = lax.all_to_all(grads, "w", 0, 0, tiled=True)
    sums = pl.pallas_call(
        functools.partial(hidden_kernel, sizes),
        grid=(nw,),
        in_specs=[
            pl.BlockSpec((1, rows, columns), lambda j: (j, 0, 0)),
            pl.BlockSpec((columns, width), lambda j: (j, 0)),
            whole((1, tokens)),
        ],
        out_specs=whole((nc, tokens // nc, lanes)),
        out_shape=jax.ShapeDtypeStruct((nc, tokens // nc, lanes), f32),
        scratch_shapes=[pltpu.VMEM((SIDE, tokens), f32)],
        compiler_params=params(),
        name="hidden_partial",
    )(grads, head_weight, shard_targets)
    sums = lax.all_to_all(sums, "c", 0, 0, tiled=True)
    sums = pl.pallas_call(
        functools.partial(cores_kernel, width),
        out_shape=jax.ShapeDtypeStruct((ny, nz * pair, lanes), i16),
        compiler_params=params(),
        name="sum_cores",
    )(sums)
    sums = lax.all_to_all(sums, "y", 0, 0, tiled=True)
    sums = pl.pallas_call(
        functools.partial(y_kernel, width),
        out_shape=jax.ShapeDtypeStruct((1, nz * pair, lanes), i16),
        compiler_params=params(),
        name="sum_y",
    )(sums)
    sums = lax.all_to_all(sums.reshape(nz, pair, lanes), "z", 0, 0, tiled=True)
    soft, hard, total = decoded(sums.reshape(nz * pair, lanes), width)
    soft = jnp.sum(soft.reshape(nz, pair, width), axis=0)
    hard = jnp.sum(hard.reshape(nz, pair, width), axis=0)
    total = jnp.sum(total.reshape(nz, pair, 1), axis=0)
    scale = lax.dynamic_slice(token_scale, (device * pair,), (pair,))[:, None]
    weighting = scale * (1.0 + 2.0 * zloss_weight * jnp.log(total))
    return (weighting / total * soft - scale * hard).astype(bf16)


def solution(mesh):
    vocab, width = mesh.devices.shape
    sizes = (4, vocab // 8, 2)
    inner = Mesh(mesh.devices.reshape(*sizes, width), ("y", "z", "c", "w"))
    vocab_axes = ("y", "z", "c")
    placed = (P(None, "w"), P(vocab_axes, "w"), P(), P())
    return jax.shard_map(
        functools.partial(on_device, sizes),
        mesh=inner,
        in_specs=placed,
        out_specs=P(vocab_axes, "w"),
        check_vma=False,
    )
```

time: 861 us -> 106 us (0.12)
  the two profiles are of different devices: /device:TPU:6 before, /device:TPU:32 now
where the time goes in v1:
time: 106 us
  blocking collectives  38.2 us (36%)
  waiting for transfers between devices  29.6 us (28%)
  starting transfers between devices  19.7 us (19%)
  Pallas kernels  10 us (9%)
  local copies, waits for them, and re-layouts  6.77 us (6%)
  other arithmetic  1.24 us (1%)
    all_to_all x1, blocking collectives, on_device(): grads = lax.all_to_all(grads, 'w', 0, 0, tiled=True)  17.3 us
    all_to_all x1, waiting for transfers between devices, on_device(): codes = lax.all_to_all(codes, 'w', 0, 0, tiled=True)  15.8 us
    all_to_all x1, starting transfers between devices, on_device(): sums = lax.all_to_all(sums.reshape(nz, pair, lanes), 'z', 0, 0, tiled=True)  15.3 us
    all_to_all x1, blocking collectives, on_device(): sums = lax.all_to_all(sums, 'y', 0, 0, tiled=True)  15.1 us
    all_to_all x1, waiting for transfers between devices, on_device(): sums = lax.all_to_all(sums.reshape(nz, pair, lanes), 'z', 0, 0, tiled=True)  13.8 us
    unnamed x10, local copies, waits for them, and re-layouts  5.74 us
    all_to_all x1, blocking collectives, on_device(): sums = lax.all_to_all(sums, 'c', 0, 0, tiled=True)  5.73 us
    pallas_call x1, Pallas kernels, on_device(): pl.pallas_call(functools.partial(hidden_kernel, sizes), grid=(nw,), in_sp...  4.73 us
  transfers between devices with their start and end apart: 2, of which 2 were waited for; matrix products, arithmetic and copies ran while one was open for 0% of the time, Pallas kernels for 0%

profile of v1, /device:TPU:32, one launch (start us, length us, event | category | flops | bytes accessed | tf_op | source)
XLA Modules:
  0.0 105.6 jit_solution(4123825309709260600)
XLA Ops:
  0.0 0.0 copy-start
  0.0 2.3 %copy-done = bf16[2048,1152]{1,0:T(8,128)(2,1)S(1)} copy-done((bf16[2048,1152]{1,0:T(8,128)(2,1)S(1)}, bf16[2048,1152]{1,0:T(8,128)(2,1)}, u32[]{:S(2)}) %copy-start) | copy-done | bytes 4718616
  2.3 0.0 copy-start.2
  2.3 1.1 %copy-done.2 = bf16[256,1152]{1,0:T(8,128)(2,1)S(1)} copy-done((bf16[256,1152]{1,0:T(8,128)(2,1)S(1)}, bf16[256,1152]{1,0:T(8,128)(2,1)}, u32[]{:S(2)}) %copy-start.2) | copy-done | bytes 589848
  3.4 3.9 %logits.1 = s16[4,272,512]{2,1,0:T(8,128)(2,1)} custom-call(bf16[256,1152]{1,0:T(8,128)(2,1)S(1)} %copy-done.2, bf16[2048,1152]{1,0:T(8,128)(2,1)S(1)} %copy-done), custom_call_target="tpu_custom_call" | custom-call | tf_op jit(solution)/shard_map/logits/pallas_call | solution.py:213
  7.3 0.0 copy-start.3
  7.3 4.4 %all-to-all-start = ((s16[4,272,512]{2,1,0:T(8,128)(2,1)}), s16[4,272,512]{2,1,0:T(8,128)(2,1)S(1)}, u32[]{:S(2)}, u32[]{:S(2)}) async-start(s16[4,272,512]{2,1,0:T(8,128)(2,1)} %logits.1), calls=%async_computation | async-start | bytes 2228224 | tf_op jit(solution)/shard_map/all_to_all | solution.py:223
  11.7 0.0 copy-done.3
  11.7 15.8 %all-to-all-done.codes_ref = s16[4,272,512]{2,1,0:T(8,128)(2,1)S(1)} async-done(((s16[4,272,512]{2,1,0:T(8,128)(2,1)}), s16[4,272,512]{2,1,0:T(8,128)(2,1)S(1)}, u32[]{:S(2)}, u32[]{:S(2)}) %all-to-all-start) | async-done | bytes 1114144 | tf_op jit(solution)/shard_map/all_to_all | solution.py:223
  27.5 0.6 exponentials.1
  28.1 17.3 %all_to_all.25.grads_ref = bf16[4,272,512]{2,1,0:T(8,128)(2,1)S(1)} all-to-all(bf16[4,272,512]{2,1,0:T(8,128)(2,1)S(1)} %exponentials.1), channel_id=1, replica_groups=mesh['y'=4,'z'=16,'c'=2,'w'=4] {'w'}, dimensions={0} | all-to-all | bytes 2228224 | tf_op jit(solution)/shard_map/all_to_all | solution.py:230
  45.4 0.0 copy-start.1
  45.4 2.3 %copy-done.1 = bf16[2048,1152]{1,0:T(8,128)(2,1)S(1)} copy-done((bf16[2048,1152]{1,0:T(8,128)(2,1)S(1)}, bf16[2048,1152]{1,0:T(8,128)(2,1)}, u32[]{:S(2)}) %copy-start.1) | copy-done | bytes 4718616
  47.8 4.7 %hidden_partial.1 = f32[2,128,2432]{2,1,0:T(8,128)S(1)} custom-call(bf16[4,272,512]{2,1,0:T(8,128)(2,1)S(1)} %all_to_all.25.grads_ref, bf16[2048,1152]{1,0:T(8,128)(2,1)S(1)} %copy-done.1, s32[1,256]{1,0:T(1,128)S(1)} %bitcast.2), custom_call_target="tpu_custom_call" | custom-call | tf_op jit(solution)/shard_map/hidden_partial/pallas_call | solution.py:231
  52.5 5.7 %all_to_all.26.in_ref = f32[2,128,2432]{2,1,0:T(8,128)S(1)} all-to-all(f32[2,128,2432]{2,1,0:T(8,128)S(1)} %hidden_partial.1), channel_id=1, replica_groups=mesh['y'=4,'z'=16,'c'=2,'w'=4] {'c'}, dimensions={0} | all-to-all | bytes 4980736 | tf_op jit(solution)/shard_map/all_to_all | solution.py:245
  58.2 0.5 sum_cores.1
  58.7 15.1 %all_to_all.27.in_ref = s16[4,32,2432]{2,1,0:T(8,128)(2,1)S(1)} all-to-all(s16[4,32,2432]{2,1,0:T(8,128)(2,1)S(1)} %sum_cores.1), channel_id=1, replica_groups=mesh['y'=4,'z'=16,'c'=2,'w'=4] {'y'}, dimensions={0} | all-to-all | bytes 1245184 | tf_op jit(solution)/shard_map/all_to_all | solution.py:252
  73.9 0.3 sum_y.1
  74.2 0.7 reshape.32
  74.9 0.0 copy-start.4
  74.9 15.3 %all-to-all-start.4 = ((s16[16,2,2432]{2,1,0:T(2,128)(2,1)}), s16[16,2,2432]{2,1,0:T(2,128)(2,1)S(1)}, u32[]{:S(2)}, u32[]{:S(2)}) async-start(s16[16,2,2432]{2,1,0:T(2,128)(2,1)} %reshape.32), calls=%async_computation.4 | async-start | bytes 311296 | tf_op jit(solution)/shard_map/all_to_all | solution.py:259
  90.2 13.8 %all-to-all-done.4 = s16[16,2,2432]{2,1,0:T(2,128)(2,1)S(1)} async-done(((s16[16,2,2432]{2,1,0:T(2,128)(2,1)}), s16[16,2,2432]{2,1,0:T(2,128)(2,1)S(1)}, u32[]{:S(2)}, u32[]{:S(2)}) %all-to-all-start.4) | async-done | bytes 155680 | tf_op jit(solution)/shard_map/all_to_all | solution.py:259
  104.0 0.1 reshape.33
  104.1 0.2 fusion.6
  104.3 0.1 reshape.34
  104.4 0.1 convert_multiply_fusion.1
  104.5 0.1 reshape.35
  104.6 0.1 reduce_sum.28
  104.7 0.1 reshape.36
  104.7 0.1 reduce_sum.29
  104.8 0.0 copy-done.4
  104.8 0.1 multiply_divide_fusion
  104.9 0.7 subtract_convert_fusion
  (3 shorter events, 0.0 us)
Async XLA Ops:
  0.0 2.3 %copy-start = (bf16[2048,1152]{1,0:T(8,128)(2,1)S(1)}, bf16[2048,1152]{1,0:T(8,128)(2,1)}, u32[]{:S(2)}) copy-start(bf16[2048,1152]{1,0:T(8,128)(2,1)} %weight_ref.3) | copy-start | bytes 14155780
  2.3 1.1 %copy-start.2 = (bf16[256,1152]{1,0:T(8,128)(2,1)S(1)}, bf16[256,1152]{1,0:T(8,128)(2,1)}, u32[]{:S(2)}) copy-start(bf16[256,1152]{1,0:T(8,128)(2,1)} %hidden_ref.1) | copy-start | bytes 1769476
  7.3 4.4 %copy-start.3 = (s32[256]{0:T(256)S(1)}, s32[256]{0:T(256)}, u32[]{:S(2)}) copy-start(s32[256]{0:T(256)} %param.6) | copy-start | bytes 3076
  7.3 20.2 %all-to-all-start = ((s16[4,272,512]{2,1,0:T(8,128)(2,1)}), s16[4,272,512]{2,1,0:T(8,128)(2,1)S(1)}, u32[]{:S(2)}, u32[]{:S(2)}) async-start(s16[4,272,512]{2,1,0:T(8,128)(2,1)} %logits.1), calls=%async_computation | async-start | bytes 2228224 | tf_op jit(solution)/shard_map/all_to_all | solution.py:223
  45.4 2.3 %copy-start.1 = (bf16[2048,1152]{1,0:T(8,128)(2,1)S(1)}, bf16[2048,1152]{1,0:T(8,128)(2,1)}, u32[]{:S(2)}) copy-start(bf16[2048,1152]{1,0:T(8,128)(2,1)} %weight_ref.3) | copy-start | bytes 14155780
  74.9 29.9 %copy-start.4 = (f32[256]{0:T(256)S(1)}, f32[256]{0:T(256)}, u32[]{:S(2)}) copy-start(f32[256]{0:T(256)} %param.7) | copy-start | bytes 3076
  74.9 29.1 %all-to-all-start.4 = ((s16[16,2,2432]{2,1,0:T(2,128)(2,1)}), s16[16,2,2432]{2,1,0:T(2,128)(2,1)S(1)}, u32[]{:S(2)}, u32[]{:S(2)}) async-start(s16[16,2,2432]{2,1,0:T(2,128)(2,1)} %reshape.32), calls=%async_computation.4 | async-start | bytes 311296 | tf_op jit(solution)/shard_map/all_to_all | solution.py:259

commit v2 on v1

v2 whole, which is shorter than its diff:
```python
import functools
import jax
import jax.numpy as jnp
from jax import lax
from jax.experimental import pallas as pl
from jax.experimental.pallas import tpu as pltpu
from jax.sharding import Mesh, PartitionSpec as P

logit_cap = 30.0
zloss_weight = 0.001

f32, bf16, i16, i32 = jnp.float32, jnp.bfloat16, jnp.int16, jnp.int32

SIDE = 16
LANES = 128
TOP = 32767.0
VMEM_BYTES = 20 * 1024 * 1024


def exponent_of(largest):
    return jnp.floor(jnp.log2(jnp.maximum(largest, 1e-30))) - 14.0


def code(values, exponent):
    scaled = jnp.floor(values * jnp.exp2(-exponent) + 0.5)
    return jnp.clip(scaled, -TOP, TOP).astype(i32).astype(i16)


def to_f32(codes):
    return codes.astype(i32).astype(f32)


def token_order(sizes, tokens):
    ny, nz, nc = sizes
    pair = tokens // (ny * nz * nc)
    place = lax.broadcasted_iota(i32, (tokens, tokens), 0)
    token = lax.broadcasted_iota(i32, (tokens, tokens), 1)
    core = place // (ny * nz * pair)
    yz = (place // pair) % (ny * nz)
    r = place % pair
    return token == (yz * nc + core) * pair + r


def column_of(mask, row):
    return jnp.sum(jnp.where(mask, row, 0.0), axis=1, keepdims=True)


def eye(n):
    return lax.broadcasted_iota(i32, (n, n), 0) == lax.broadcasted_iota(i32, (n, n), 1)


def rows_of(part, columns):
    return pl.ds(pl.multiple_of(part * columns, columns), columns)


def coded_logits(ordered, weight, out_ref):
    tokens = ordered.shape[0]
    partial = raw_part(ordered, weight)
    exponent = exponent_of(jnp.max(jnp.abs(partial), axis=0, keepdims=True))
    out_ref[0:tokens, :] = code(partial, exponent)
    out_ref[tokens:, :] = jnp.broadcast_to(
        exponent, (SIDE, exponent.shape[1])
    ).astype(i32).astype(i16)


def raw_part(ordered, weight):
    return lax.dot_general(ordered, weight, (((1,), (1,)), ((), ())), preferred_element_type=f32)


def far_logits_kernel(
    sizes, parts, hidden_hbm, weight_hbm, targets_hbm, scale_hbm,
    out_ref, ordered_ref, place_ref, own_scale_ref,
    hidden_ref, weight_ref, targets_ref, scale_ref, sems,
):
    tokens = hidden_ref.shape[0]
    pair = own_scale_ref.shape[0]
    columns = out_ref.shape[1]
    far = lax.rem(lax.axis_index("w") + parts // 2, parts)
    copies = [
        pltpu.make_async_copy(source, target, sems.at[at])
        for at, (source, target) in enumerate(
            (
                (hidden_hbm, hidden_ref),
                (targets_hbm, targets_ref),
                (scale_hbm, scale_ref),
                (weight_hbm.at[rows_of(far, columns)], weight_ref),
            )
        )
    ]
    for copy in copies:
        copy.start()
    ordering = token_order(sizes, tokens)
    order = jnp.where(ordering, 1.0, 0.0).astype(bf16)
    ny, nz, nc = sizes
    device = (lax.axis_index("y") * nz + lax.axis_index("z")) * nc + lax.axis_index("c")
    copies[0].wait()
    ordered = jnp.dot(order, hidden_ref[...], preferred_element_type=f32).astype(bf16)
    ordered_ref[...] = ordered
    copies[1].wait()
    place = column_of(ordering, (targets_ref[...] - device * (parts * columns)).astype(f32))
    place_ref[...] = jnp.broadcast_to(place, place_ref.shape)
    copies[2].wait()
    mine = lax.broadcasted_iota(i32, (pair, tokens), 1) == (
        device * pair + lax.broadcasted_iota(i32, (pair, tokens), 0)
    )
    own_scale_ref[...] = jnp.broadcast_to(column_of(mine, scale_ref[...]), own_scale_ref.shape)
    copies[3].wait()
    coded_logits(ordered, weight_ref[...], out_ref)


def near_logits_kernel(
    parts, steps, ordered_ref, weight_hbm, *refs
):
    out_refs, own_ref, weight_ref, sems = refs[: len(steps)], refs[-3], refs[-2], refs[-1]
    columns = own_ref.shape[1]
    me = lax.axis_index("w")
    copies = [
        pltpu.make_async_copy(
            weight_hbm.at[rows_of(lax.rem(me + step, parts), columns)],
            weight_ref.at[at],
            sems.at[at],
        )
        for at, step in enumerate((*steps, 0))
    ]
    for copy in copies:
        copy.start()
    ordered = ordered_ref[...]
    for at, out_ref in enumerate(out_refs):
        copies[at].wait()
        coded_logits(ordered, weight_ref[at], out_ref)
    copies[-1].wait()
    own_ref[...] = raw_part(ordered, weight_ref[len(steps)])


def exp_kernel(own_ref, *refs):
    codes_refs, place_ref, out_ref = refs[:-2], refs[-2], refs[-1]
    tokens, columns = own_ref.shape
    raw = own_ref[...]
    for codes_ref in codes_refs:
        exponent = to_f32(codes_ref[tokens:, :])[0:1]
        raw = raw + to_f32(codes_ref[0:tokens, :]) * jnp.exp2(exponent)
    tangent = jnp.tanh(raw / logit_cap)
    exp_terms = jnp.exp(logit_cap * tangent)
    slope = 1.0 - tangent * tangent
    sums = jnp.sum(exp_terms, axis=1, keepdims=True)
    targets = place_ref[:, 0:1]
    places = lax.broadcasted_iota(i32, raw.shape, 1) + lax.axis_index("w") * columns
    at_target = jnp.sum(
        jnp.where(targets == places.astype(f32), slope, 0.0), axis=1, keepdims=True
    )
    diagonal = eye(tokens)
    sum_row = jnp.sum(jnp.where(diagonal, sums, 0.0), axis=0, keepdims=True)
    target_row = jnp.sum(jnp.where(diagonal, at_target, 0.0), axis=0, keepdims=True)
    which = lax.broadcasted_iota(i32, (SIDE, tokens), 0)
    side = jnp.where(which == 0, sum_row, jnp.where(which == 1, target_row, 0.0))
    high = side.astype(bf16)
    low = (side - high.astype(f32)).astype(bf16)
    pieces = [high, low]
    if columns > 2 * tokens:
        pieces.append(jnp.zeros((SIDE, columns - 2 * tokens), bf16))
    out_ref[0:tokens, :] = (exp_terms * slope).astype(bf16)
    out_ref[tokens:, :] = jnp.concatenate(pieces, axis=1)


def side_of(grads_ref, tokens):
    side = grads_ref[tokens:, :].astype(f32)
    return side[:, 0:tokens] + side[:, tokens : 2 * tokens]


def own_hidden_kernel(
    parts, grads_ref, weight_hbm, place_ref, soft_ref, hard_ref, side_ref, weight_ref, sems
):
    tokens, _ = soft_ref.shape
    columns = grads_ref.shape[1]
    me = lax.axis_index("w")
    order = [lax.rem(me + step, parts) for step in range(parts)]
    copies = [
        pltpu.make_async_copy(
            weight_hbm.at[rows_of(part, columns)], weight_ref.at[rows_of(part, columns)], sems.at[at]
        )
        for at, part in enumerate(order)
    ]
    for copy in copies:
        copy.start()
    targets = place_ref[:, 0:1]
    lane = lax.broadcasted_iota(i32, (tokens, columns), 1)
    side_ref[...] = side_of(grads_ref, tokens)
    hard = None
    for at, part in enumerate(order):
        at_target = targets == (lane + part * columns).astype(f32)
        at_target = jnp.where(at_target, 1.0, 0.0).astype(bf16)
        copies[at].wait()
        weight = weight_ref[rows_of(part, columns)]
        if at == 0:
            soft_ref[...] = jnp.dot(
                grads_ref[0:tokens, :], weight, preferred_element_type=f32
            )
        term = jnp.dot(at_target, weight, preferred_element_type=f32)
        hard = term if hard is None else hard + term
    hard_ref[...] = hard


def near_hidden_kernel(parts, steps, soft_ref, side_ref, weight_ref, *refs):
    grads_refs, out_ref, out_side_ref = refs[:-2], refs[-2], refs[-1]
    tokens = soft_ref.shape[0]
    me = lax.axis_index("w")
    soft, side = soft_ref[...], side_ref[...]
    for step, grads_ref in zip(steps, grads_refs, strict=True):
        columns = grads_ref.shape[1]
        weight = weight_ref[rows_of(lax.rem(me + parts - step, parts), columns)]
        soft = soft + jnp.dot(grads_ref[0:tokens, :], weight, preferred_element_type=f32)
        side = side + side_of(grads_ref, tokens)
    out_ref[...] = soft
    out_side_ref[...] = side


def far_hidden_kernel(
    parts, soft_ref, side_ref, weight_ref, hard_ref, grads_ref, mine_ref, other_ref, sum_ref
):
    tokens, width = soft_ref.shape
    own = mine_ref.shape[0]
    columns = grads_ref.shape[1]
    far = lax.rem(lax.axis_index("w") + parts // 2, parts)
    weight = weight_ref[rows_of(far, columns)]
    soft = soft_ref[...] + jnp.dot(
        grads_ref[0:tokens, :], weight, preferred_element_type=f32
    )
    side = side_ref[...] + side_of(grads_ref, tokens)
    diagonal = eye(tokens)
    sums = column_of(diagonal, side[0:1, :])
    slope = column_of(diagonal, side[1:2, :])
    sum_ref[:, 0:width] = soft
    sum_ref[:, width : 2 * width] = hard_ref[...] * slope
    sum_ref[:, 2 * width :] = jnp.broadcast_to(sums, (tokens, LANES))
    core = lax.axis_index("c")
    mine_ref[...] = sum_ref[rows_of(core, own)]
    other_ref[...] = sum_ref[rows_of(1 - core, own)]


def coded_rows(soft, hard, total):
    rows = soft.shape[0]
    soft_exp = exponent_of(jnp.max(jnp.abs(soft), axis=1, keepdims=True))
    hard_exp = exponent_of(jnp.max(jnp.abs(hard), axis=1, keepdims=True))
    total_exp = jnp.floor(jnp.log2(jnp.maximum(total, 1e-30))) - 24.0
    scaled = total * jnp.exp2(-total_exp)
    high = jnp.floor(scaled * (1.0 / 4096.0))
    low = scaled - high * 4096.0
    lane = lax.broadcasted_iota(i32, (rows, LANES), 1)
    side = jnp.where(lane == 0, soft_exp, 0.0)
    for at, value in enumerate((hard_exp, total_exp, high, low), 1):
        side = jnp.where(lane == at, value, side)
    side = side.astype(i32).astype(i16)
    return code(soft, soft_exp), code(hard, hard_exp), side


def decoded(codes, width):
    side = to_f32(codes[:, 2 * width :])
    soft = to_f32(codes[:, 0:width]) * jnp.exp2(side[:, 0:1])
    hard = to_f32(codes[:, width : 2 * width]) * jnp.exp2(side[:, 1:2])
    total = (side[:, 3:4] * 4096.0 + side[:, 4:5]) * jnp.exp2(side[:, 2:3])
    return soft, hard, total


def store_rows(out_ref, soft, hard, total, width):
    parts, rows, _ = out_ref.shape
    coded = coded_rows(soft, hard, total)
    at = 0
    for piece in coded:
        for part in range(parts):
            out_ref[part, :, at : at + piece.shape[1]] = piece[part * rows : (part + 1) * rows]
        at += piece.shape[1]


def cores_kernel(width, mine_ref, other_ref, out_ref):
    total = mine_ref[...] + other_ref[...]
    soft, hard = total[:, 0:width], total[:, width : 2 * width]
    store_rows(out_ref, soft, hard, total[:, 2 * width : 2 * width + 1], width)


def y_kernel(width, in_ref, out_ref):
    terms = [decoded(in_ref[part], width) for part in range(in_ref.shape[0])]
    soft, hard, total = (functools.reduce(jnp.add, t) for t in zip(*terms))
    store_rows(out_ref, soft, hard, total, width)


def z_kernel(width, in_ref, scale_ref, out_ref):
    terms = [decoded(in_ref[part], width) for part in range(in_ref.shape[0])]
    soft, hard, total = (functools.reduce(jnp.add, t) for t in zip(*terms))
    scale = scale_ref[:, 0:1]
    weighting = scale * (1.0 + 2.0 * zloss_weight * jnp.log(total))
    out_ref[...] = (weighting / total * soft - scale * hard).astype(bf16)


def params():
    return pltpu.CompilerParams(vmem_limit_bytes=VMEM_BYTES)


def on_device(sizes, hidden, head_weight, targets, token_scale):
    ny, nz, nc = sizes
    nw = lax.axis_size("w")
    tokens, width = hidden.shape
    vocab = head_weight.shape[0]
    columns = vocab // nw
    rows = tokens + SIDE
    pair = tokens // (ny * nz * nc)
    lanes = 2 * width + LANES
    hbm = pl.BlockSpec(memory_space=pltpu.HBM)
    vmem = pl.BlockSpec(memory_space=pltpu.VMEM)
    steps = tuple(k for k in range(1, nw) if k != nw // 2)

    def shape(*dims, dtype=f32):
        return jax.ShapeDtypeStruct(dims, dtype)

    def send(x, step):
        return lax.ppermute(x, "w", [(i, (i + step) % nw) for i in range(nw)])

    in_hbm = functools.partial(pltpu.with_memory_space_constraint, memory_space=pltpu.HBM)
    weight_hbm = in_hbm(head_weight)
    far, ordered, place, scale = pl.pallas_call(
        functools.partial(far_logits_kernel, sizes, nw),
        in_specs=[hbm] * 4,
        out_specs=[vmem] * 4,
        out_shape=[
            shape(rows, columns, dtype=i16),
            shape(tokens, width, dtype=bf16),
            shape(tokens, LANES),
            shape(pair, LANES),
        ],
        scratch_shapes=[
            pltpu.VMEM((tokens, width), bf16),
            pltpu.VMEM((columns, width), bf16),
            pltpu.VMEM((1, tokens), i32),
            pltpu.VMEM((1, tokens), f32),
            pltpu.SemaphoreType.DMA((4,)),
        ],
        compiler_params=params(),
        name="far_logits",
    )(
        in_hbm(hidden),
        weight_hbm,
        in_hbm(targets.reshape(1, tokens)),
        in_hbm(token_scale.reshape(1, tokens)),
    )
    far = send(far, nw // 2)
    *near, own = pl.pallas_call(
        functools.partial(near_logits_kernel, nw, steps),
        in_specs=[vmem, hbm],
        out_specs=[vmem] * (len(steps) + 1),
        out_shape=[shape(rows, columns, dtype=i16)] * len(steps) + [shape(tokens, columns)],
        scratch_shapes=[
            pltpu.VMEM((len(steps) + 1, columns, width), bf16),
            pltpu.SemaphoreType.DMA((len(steps) + 1,)),
        ],
        compiler_params=params(),
        name="near_logits",
    )(ordered, weight_hbm)
    near = [send(x, step) for x, step in zip(near, steps, strict=True)]
    grads = pl.pallas_call(
        exp_kernel,
        out_shape=shape(rows, columns, dtype=bf16),
        compiler_params=params(),
        name="exponentials",
    )(own, far, *near, place)
    far = send(grads, nw // 2)
    near = [send(grads, step) for step in steps]
    soft, hard, side, weight = pl.pallas_call(
        functools.partial(own_hidden_kernel, nw),
        in_specs=[vmem, hbm, vmem],
        out_specs=[vmem] * 4,
        out_shape=[
            shape(tokens, width),
            shape(tokens, width),
            shape(SIDE, tokens),
            shape(vocab, width, dtype=bf16),
        ],
        scratch_shapes=[pltpu.SemaphoreType.DMA((nw,))],
        compiler_params=params(),
        name="own_hidden",
    )(grads, weight_hbm, place)
    soft, side = pl.pallas_call(
        functools.partial(near_hidden_kernel, nw, steps),
        out_shape=[shape(tokens, width), shape(SIDE, tokens)],
        compiler_params=params(),
        name="near_hidden",
    )(soft, side, weight, *near)
    mine, other = pl.pallas_call(
        functools.partial(far_hidden_kernel, nw),
        out_shape=[shape(tokens // nc, lanes)] * 2,
        scratch_shapes=[pltpu.VMEM((tokens, lanes), f32)],
        compiler_params=params(),
        name="far_hidden",
    )(soft, side, weight, hard, far)
    other = lax.ppermute(other, "c", [(0, 1), (1, 0)])
    sums = pl.pallas_call(
        functools.partial(cores_kernel, width),
        out_shape=jax.ShapeDtypeStruct((ny, nz * pair, lanes), i16),
        compiler_params=params(),
        name="sum_cores",
    )(mine, other)
    sums = lax.all_to_all(sums, "y", 0, 0, tiled=True)
    sums = pl.pallas_call(
        functools.partial(y_kernel, width),
        out_shape=jax.ShapeDtypeStruct((nz, pair, lanes), i16),
        compiler_params=params(),
        name="sum_y",
    )(sums)
    sums = lax.all_to_all(sums, "z", 0, 0, tiled=True)
    return pl.pallas_call(
        functools.partial(z_kernel, width),
        out_shape=jax.ShapeDtypeStruct((pair, width), bf16),
        compiler_params=params(),
        name="sum_z",
    )(sums, scale)


def solution(mesh):
    vocab, width = mesh.devices.shape
    sizes = (4, vocab // 8, 2)
    inner = Mesh(mesh.devices.reshape(*sizes, width), ("y", "z", "c", "w"))
    vocab_axes = ("y", "z", "c")
    placed = (P(None, "w"), P(vocab_axes, "w"), P(), P())
    return jax.shard_map(
        functools.partial(on_device, sizes),
        mesh=inner,
        in_specs=placed,
        out_specs=P(vocab_axes, "w"),
        check_vma=False,
    )
```

time: 106 us -> 97.3 us (0.918)
  waiting for transfers between devices: 29.6 us -> 14.9 us
  local copies, waits for them, and re-layouts: 6.77 us -> 0 us
  blocking collectives: 38.2 us -> 43.9 us
  starting transfers between devices: 19.7 us -> 24.8 us
  Pallas kernels: 10 us -> 13.1 us
  other arithmetic: 1.24 us -> 0 us
    all_to_all x2 -> x0, waiting for transfers between devices: 29.6 us -> none  [the longest x1 15.8 us: on_device(): codes = lax.all_to_all(codes, 'w', 0, 0, tiled=True)]
    ppermute x0 -> x7, starting transfers between devices: none -> 24.8 us  [the longest x6 22.9 us: send(): return lax.ppermute(x, 'w', [(i, (i + step) % nw) for i in range(nw)])]
    all_to_all x2 -> x0, starting transfers between devices: 19.7 us -> none  [the longest x1 15.3 us: on_device(): sums = lax.all_to_all(sums.reshape(nz, pair, lanes), 'z', 0, 0, tiled=True)]
    ppermute x0 -> x7, waiting for transfers between devices: none -> 14.9 us  [the longest x6 12 us: send(): return lax.ppermute(x, 'w', [(i, (i + step) % nw) for i in range(nw)])]
    all_to_all x2 -> x1, blocking collectives: 23 us -> 28.8 us  [on_device(): sums = lax.all_to_all(sums, 'z', 0, 0, tiled=True)]
    unnamed x10 -> x0, local copies, waits for them, and re-layouts: 5.74 us -> none
    pallas_call x3 -> x7, Pallas kernels: 9.22 us -> 12.3 us  [the longest x1 3.71 us: on_device(): pl.pallas_call(functools.partial(own_hidden_kernel, nw), in_specs=[vmem,...]
  transfers between devices with their start and end apart: 2 -> 7, of which waited for: 2 -> 4; matrix products, arithmetic and copies ran while one was open for 0% -> 0% of each run, Pallas kernels for 0% -> 8%
where the time goes in v2:
time: 97.3 us; the launch traced here: 96.9 us
  blocking collectives  43.9 us (45%)
  starting transfers between devices  24.8 us (25%)
  waiting for transfers between devices  14.9 us (15%)
  Pallas kernels  13.1 us (13%)
    all_to_all x1, blocking collectives, on_device(): sums = lax.all_to_all(sums, 'z', 0, 0, tiled=True)  28.8 us
    ppermute x6, starting transfers between devices, send(): return lax.ppermute(x, 'w', [(i, (i + step) % nw) for i in range(nw)])  22.9 us
    all_to_all x1, blocking collectives, on_device(): sums = lax.all_to_all(sums, 'y', 0, 0, tiled=True)  15.1 us
    ppermute x6, waiting for transfers between devices, send(): return lax.ppermute(x, 'w', [(i, (i + step) % nw) for i in range(nw)])  12 us
    pallas_call x1, Pallas kernels, on_device(): pl.pallas_call(functools.partial(own_hidden_kernel, nw), in_specs=[vmem,...  3.71 us
    pallas_call x1, Pallas kernels, on_device(): pl.pallas_call(functools.partial(near_logits_kernel, nw, steps), in_specs...  3.21 us
    ppermute x1, waiting for transfers between devices, on_device(): other = lax.ppermute(other, 'c', [(0, 1), (1, 0)])  2.91 us
    pallas_call x1, Pallas kernels, on_device(): pl.pallas_call(functools.partial(far_logits_kernel, sizes, nw), in_specs=...  2.32 us
  transfers between devices with their start and end apart: 7, of which 4 were waited for; matrix products, arithmetic and copies ran while one was open for 0% of the time, Pallas kernels for 8%

profile of v2, /device:TPU:32, one launch (start us, length us, event | category | flops | bytes accessed | tf_op | source)
XLA Modules:
  0.0 96.9 jit_solution(4971485970057107349)
XLA Ops:
  0.0 2.3 %far_logits.1 = (s16[272,512]{1,0:T(8,128)(2,1)S(1)}, bf16[256,1152]{1,0:T(8,128)(2,1)S(1)}, f32[256,128]{1,0:T(8,128)S(1)}, f32[2,128]{1,0:T(2,128)S(1)}) custom-call(bf16[256,1152]{1,0:T(8,128)(2,1)} %hidden_hbm.1, bf16[2048,1152]{1,0:T(8,128)(2,1)} %weight_hbm.5, s32[1,256]{1,0:T(1,128)} %bitcast.2, f32[1,256]{1,0:T(1,128)} %bitcast.3), custom_call_target="tpu_custom_call" | custom-call | tf_op jit(solution)/shard_map/far_logits/pallas_call | solution.py:319
  2.3 4.9 %collective-permute-start = (s16[272,512]{1,0:T(8,128)(2,1)S(1)}, s16[272,512]{1,0:T(8,128)(2,1)S(1)}, u32[]{:S(2)}, u32[]{:S(2)}) collective-permute-start(s16[272,512]{1,0:T(8,128)(2,1)S(1)} %get-tuple-element.22), channel_id=1, source_target_pairs={{0,2},{1,3},{2,0},{3,1},{4,6},{5,7},{6,4},{7,5},{8,10},{9,11},{10,... | collective-permute-start | bytes 835592 | tf_op jit(solution)/shard_map/ppermute | solution.py:315
  7.3 3.2 %near_logits.1 = (s16[272,512]{1,0:T(8,128)(2,1)S(1)}, s16[272,512]{1,0:T(8,128)(2,1)S(1)}, f32[256,512]{1,0:T(8,128)S(1)}) custom-call(bf16[256,1152]{1,0:T(8,128)(2,1)S(1)} %get-tuple-element.20.ordered_ref, bf16[2048,1152]{1,0:T(8,128)(2,1)} %weight_hbm.5), custom_call_target="tpu_custom_call" | custom-call | tf_op jit(solution)/shard_map/near_logits/pallas_call | solution.py:345
  10.5 2.5 %collective-permute-start.1 = (s16[272,512]{1,0:T(8,128)(2,1)S(1)}, s16[272,512]{1,0:T(8,128)(2,1)S(1)}, u32[]{:S(2)}, u32[]{:S(2)}) collective-permute-start(s16[272,512]{1,0:T(8,128)(2,1)S(1)} %get-tuple-element.23), channel_id=1, source_target_pairs={{0,1},{1,2},{2,3},{3,0},{4,5},{5,6},{6,7},{7,4},{8,9},{9,10},{10,1... | collective-permute-start | bytes 835592 | tf_op jit(solution)/shard_map/ppermute | solution.py:315
  13.0 4.6 %collective-permute-start.2 = (s16[272,512]{1,0:T(8,128)(2,1)S(1)}, s16[272,512]{1,0:T(8,128)(2,1)S(1)}, u32[]{:S(2)}, u32[]{:S(2)}) collective-permute-start(s16[272,512]{1,0:T(8,128)(2,1)S(1)} %get-tuple-element.24), channel_id=1, source_target_pairs={{0,3},{1,0},{2,1},{3,2},{4,7},{5,4},{6,5},{7,6},{8,11},{9,8},{10,9... | collective-permute-start | bytes 835592 | tf_op jit(solution)/shard_map/ppermute | solution.py:315
  17.6 0.0 collective-permute-done.refs_0_
  17.6 4.1 %collective-permute-done.1.refs_1_ = s16[272,512]{1,0:T(8,128)(2,1)S(1)} collective-permute-done((s16[272,512]{1,0:T(8,128)(2,1)S(1)}, s16[272,512]{1,0:T(8,128)(2,1)S(1)}, u32[]{:S(2)}, u32[]{:S(2)}) %collective-permute-start.1) | collective-permute-done | bytes 278560 | tf_op jit(solution)/shard_map/ppermute | solution.py:315
  21.7 1.2 %collective-permute-done.2.refs_2_ = s16[272,512]{1,0:T(8,128)(2,1)S(1)} collective-permute-done((s16[272,512]{1,0:T(8,128)(2,1)S(1)}, s16[272,512]{1,0:T(8,128)(2,1)S(1)}, u32[]{:S(2)}, u32[]{:S(2)}) %collective-permute-start.2) | collective-permute-done | bytes 278560 | tf_op jit(solution)/shard_map/ppermute | solution.py:315
  22.9 0.6 exponentials.1.grads_ref
  23.5 5.6 %collective-permute-start.4 = (bf16[272,512]{1,0:T(8,128)(2,1)S(1)}, bf16[272,512]{1,0:T(8,128)(2,1)S(1)}, u32[]{:S(2)}, u32[]{:S(2)}) collective-permute-start(bf16[272,512]{1,0:T(8,128)(2,1)S(1)} %exponentials.1.grads_ref), channel_id=1, source_target_pairs={{0,3},{1,0},{2,1},{3,2},{4,7},{5,4},{6,5},{7,6},{8,11},{9,8},{10,9... | collective-permute-start | bytes 835592 | tf_op jit(solution)/shard_map/ppermute | solution.py:315
  29.1 1.9 %collective-permute-start.3 = (bf16[272,512]{1,0:T(8,128)(2,1)S(1)}, bf16[272,512]{1,0:T(8,128)(2,1)S(1)}, u32[]{:S(2)}, u32[]{:S(2)}) collective-permute-start(bf16[272,512]{1,0:T(8,128)(2,1)S(1)} %exponentials.1.grads_ref), channel_id=1, source_target_pairs={{0,1},{1,2},{2,3},{3,0},{4,5},{5,6},{6,7},{7,4},{8,9},{9,10},{10,1... | collective-permute-start | bytes 835592 | tf_op jit(solution)/shard_map/ppermute | solution.py:315
  31.0 3.4 %collective-permute-start.5 = (bf16[272,512]{1,0:T(8,128)(2,1)S(1)}, bf16[272,512]{1,0:T(8,128)(2,1)S(1)}, u32[]{:S(2)}, u32[]{:S(2)}) collective-permute-start(bf16[272,512]{1,0:T(8,128)(2,1)S(1)} %exponentials.1.grads_ref), channel_id=1, source_target_pairs={{0,2},{1,3},{2,0},{3,1},{4,6},{5,7},{6,4},{7,5},{8,10},{9,11},{10,... | collective-permute-start | bytes 835592 | tf_op jit(solution)/shard_map/ppermute | solution.py:315
  34.4 3.7 %own_hidden.1 = (f32[256,1152]{1,0:T(8,128)S(1)}, f32[256,1152]{1,0:T(8,128)S(1)}, f32[16,256]{1,0:T(8,128)S(1)}, bf16[2048,1152]{1,0:T(8,128)(2,1)S(1)}) custom-call(bf16[272,512]{1,0:T(8,128)(2,1)S(1)} %exponentials.1.grads_ref, bf16[2048,1152]{1,0:T(8,128)(2,1)} %weight_hbm.5, f32[256,128]{1,0:T(8,128)S(1)} %get-tuple-element.25.refs_3_.place_ref), custom_call_target="tpu_custom_call" | custom-call | tf_op jit(solution)/shard_map/own_hidden/pallas_call | solution.py:366
  38.1 0.0 collective-permute-done.4.refs_1_
  38.1 6.7 %collective-permute-done.3.refs_0_ = bf16[272,512]{1,0:T(8,128)(2,1)S(1)} collective-permute-done((bf16[272,512]{1,0:T(8,128)(2,1)S(1)}, bf16[272,512]{1,0:T(8,128)(2,1)S(1)}, u32[]{:S(2)}, u32[]{:S(2)}) %collective-permute-start.3) | collective-permute-done | bytes 278560 | tf_op jit(solution)/shard_map/ppermute | solution.py:315
  44.8 0.8 near_hidden.1
  45.6 0.0 collective-permute-done.5.grads_ref
  45.6 0.8 far_hidden.1
  46.4 1.9 %collective-permute-start.6 = (f32[128,2432]{1,0:T(8,128)S(1)}, f32[128,2432]{1,0:T(8,128)S(1)}, u32[]{:S(2)}, u32[]{:S(2)}) collective-permute-start(f32[128,2432]{1,0:T(8,128)S(1)} %get-tuple-element.33), channel_id=1, source_target_pairs={{0,4},{4,0},{1,5},{5,1},{2,6},{6,2},{3,7},{7,3},{8,12},{12,8},{9,1... | collective-permute-start | bytes 3735560 | tf_op jit(solution)/shard_map/ppermute | solution.py:393
  48.4 2.9 %collective-permute-done.6.other_ref = f32[128,2432]{1,0:T(8,128)S(1)} collective-permute-done((f32[128,2432]{1,0:T(8,128)S(1)}, f32[128,2432]{1,0:T(8,128)S(1)}, u32[]{:S(2)}, u32[]{:S(2)}) %collective-permute-start.6) | collective-permute-done | bytes 1245216 | tf_op jit(solution)/shard_map/ppermute | solution.py:393
  51.3 0.5 sum_cores.1
  51.8 15.1 %all_to_all.10.in_ref = s16[4,32,2432]{2,1,0:T(8,128)(2,1)S(1)} all-to-all(s16[4,32,2432]{2,1,0:T(8,128)(2,1)S(1)} %sum_cores.1), channel_id=1, replica_groups=mesh['y'=4,'z'=16,'c'=2,'w'=4] {'y'}, dimensions={0} | all-to-all | bytes 1245184 | tf_op jit(solution)/shard_map/all_to_all | solution.py:400
  66.9 0.3 sum_y.1
  67.2 28.8 %all_to_all.11.in_ref = s16[16,2,2432]{2,1,0:T(2,128)(2,1)S(1)} all-to-all(s16[16,2,2432]{2,1,0:T(2,128)(2,1)S(1)} %sum_y.1), channel_id=1, replica_groups=mesh['y'=4,'z'=16,'c'=2,'w'=4] {'z'}, dimensions={0} | all-to-all | bytes 311296 | tf_op jit(solution)/shard_map/all_to_all | solution.py:407
  96.0 0.9 sum_z.1
Async XLA Ops:
  2.3 15.2 %collective-permute-start = (s16[272,512]{1,0:T(8,128)(2,1)S(1)}, s16[272,512]{1,0:T(8,128)(2,1)S(1)}, u32[]{:S(2)}, u32[]{:S(2)}) collective-permute-start(s16[272,512]{1,0:T(8,128)(2,1)S(1)} %get-tuple-element.22), channel_id=1, source_target_pairs={{0,2},{1,3},{2,0},{3,1},{4,6},{5,7},{6,4},{7,5},{8,10},{9,11},{10,... | collective-permute-start | bytes 835592 | tf_op jit(solution)/shard_map/ppermute | solution.py:315
  10.5 11.2 %collective-permute-start.1 = (s16[272,512]{1,0:T(8,128)(2,1)S(1)}, s16[272,512]{1,0:T(8,128)(2,1)S(1)}, u32[]{:S(2)}, u32[]{:S(2)}) collective-permute-start(s16[272,512]{1,0:T(8,128)(2,1)S(1)} %get-tuple-element.23), channel_id=1, source_target_pairs={{0,1},{1,2},{2,3},{3,0},{4,5},{5,6},{6,7},{7,4},{8,9},{9,10},{10,1... | collective-permute-start | bytes 835592 | tf_op jit(solution)/shard_map/ppermute | solution.py:315
  13.0 9.9 %collective-permute-start.2 = (s16[272,512]{1,0:T(8,128)(2,1)S(1)}, s16[272,512]{1,0:T(8,128)(2,1)S(1)}, u32[]{:S(2)}, u32[]{:S(2)}) collective-permute-start(s16[272,512]{1,0:T(8,128)(2,1)S(1)} %get-tuple-element.24), channel_id=1, source_target_pairs={{0,3},{1,0},{2,1},{3,2},{4,7},{5,4},{6,5},{7,6},{8,11},{9,8},{10,9... | collective-permute-start | bytes 835592 | tf_op jit(solution)/shard_map/ppermute | solution.py:315
  23.5 14.6 %collective-permute-start.4 = (bf16[272,512]{1,0:T(8,128)(2,1)S(1)}, bf16[272,512]{1,0:T(8,128)(2,1)S(1)}, u32[]{:S(2)}, u32[]{:S(2)}) collective-permute-start(bf16[272,512]{1,0:T(8,128)(2,1)S(1)} %exponentials.1.grads_ref), channel_id=1, source_target_pairs={{0,3},{1,0},{2,1},{3,2},{4,7},{5,4},{6,5},{7,6},{8,11},{9,8},{10,9... | collective-permute-start | bytes 835592 | tf_op jit(solution)/shard_map/ppermute | solution.py:315
  29.1 15.7 %collective-permute-start.3 = (bf16[272,512]{1,0:T(8,128)(2,1)S(1)}, bf16[272,512]{1,0:T(8,128)(2,1)S(1)}, u32[]{:S(2)}, u32[]{:S(2)}) collective-permute-start(bf16[272,512]{1,0:T(8,128)(2,1)S(1)} %exponentials.1.grads_ref), channel_id=1, source_target_pairs={{0,1},{1,2},{2,3},{3,0},{4,5},{5,6},{6,7},{7,4},{8,9},{9,10},{10,1... | collective-permute-start | bytes 835592 | tf_op jit(solution)/shard_map/ppermute | solution.py:315
  31.0 14.6 %collective-permute-start.5 = (bf16[272,512]{1,0:T(8,128)(2,1)S(1)}, bf16[272,512]{1,0:T(8,128)(2,1)S(1)}, u32[]{:S(2)}, u32[]{:S(2)}) collective-permute-start(bf16[272,512]{1,0:T(8,128)(2,1)S(1)} %exponentials.1.grads_ref), channel_id=1, source_target_pairs={{0,2},{1,3},{2,0},{3,1},{4,6},{5,7},{6,4},{7,5},{8,10},{9,11},{10,... | collective-permute-start | bytes 835592 | tf_op jit(solution)/shard_map/ppermute | solution.py:315
  46.4 4.8 %collective-permute-start.6 = (f32[128,2432]{1,0:T(8,128)S(1)}, f32[128,2432]{1,0:T(8,128)S(1)}, u32[]{:S(2)}, u32[]{:S(2)}) collective-permute-start(f32[128,2432]{1,0:T(8,128)S(1)} %get-tuple-element.33), channel_id=1, source_target_pairs={{0,4},{4,0},{1,5},{5,1},{2,6},{6,2},{3,7},{7,3},{8,12},{12,8},{9,1... | collective-permute-start | bytes 3735560 | tf_op jit(solution)/shard_map/ppermute | solution.py:393

commit v3 on v1

v3 whole, which is shorter than its diff:
```python
import functools
import jax
import jax.numpy as jnp
from jax import lax
from jax.experimental import pallas as pl
from jax.experimental.pallas import tpu as pltpu
from jax.sharding import Mesh, PartitionSpec as P

logit_cap = 30.0
zloss_weight = 0.001

f32, bf16, i16, i32 = jnp.float32, jnp.bfloat16, jnp.int16, jnp.int32

SIDE = 16
LANES = 128
TOP = 32767.0
VMEM_BYTES = 18 * 1024 * 1024


def exponent_of(largest):
    return jnp.floor(jnp.log2(jnp.maximum(largest, 1e-30))) - 14.0


def code(values, exponent):
    scaled = jnp.floor(values * jnp.exp2(-exponent) + 0.5)
    return jnp.clip(scaled, -TOP, TOP).astype(i32).astype(i16)


def to_f32(codes):
    return codes.astype(i32).astype(f32)


def token_order(sizes, tokens):
    ny, nz, nc = sizes
    pair = tokens // (ny * nz * nc)
    place = lax.broadcasted_iota(i32, (tokens, tokens), 0)
    token = lax.broadcasted_iota(i32, (tokens, tokens), 1)
    core = place // (ny * nz * pair)
    yz = (place // pair) % (ny * nz)
    r = place % pair
    return token == (yz * nc + core) * pair + r


def column_of(mask, row):
    return jnp.sum(jnp.where(mask, row, 0.0), axis=1, keepdims=True)


def eye(n):
    return lax.broadcasted_iota(i32, (n, n), 0) == lax.broadcasted_iota(i32, (n, n), 1)


def rows_of(part, columns):
    return pl.ds(pl.multiple_of(part * columns, columns), columns)


def coded_logits(ordered, weight, out_ref):
    tokens = ordered.shape[0]
    partial = lax.dot_general(
        ordered, weight, (((1,), (1,)), ((), ())), preferred_element_type=f32
    )
    exponent = exponent_of(jnp.max(jnp.abs(partial), axis=0, keepdims=True))
    out_ref[0:tokens, :] = code(partial, exponent)
    out_ref[tokens:, :] = jnp.broadcast_to(
        exponent, (SIDE, exponent.shape[1])
    ).astype(i32).astype(i16)


def logits_kernel(
    sizes, hidden_hbm, weight_hbm, targets_hbm, scale_hbm,
    out_ref, place_ref, own_scale_ref, hard_ref, weight_ref,
    hidden_ref, part_ref, targets_ref, scale_ref, sems, weight_sems,
):
    tokens = hidden_ref.shape[0]
    pair = own_scale_ref.shape[0]
    parts, _, columns = out_ref.shape
    sources = [(hidden_hbm, hidden_ref), (targets_hbm, targets_ref), (scale_hbm, scale_ref)]
    for part in range(parts):
        sources.append((weight_hbm.at[pl.ds(part * columns, columns)], part_ref.at[part]))
    copies = [
        pltpu.make_async_copy(source, target, sems.at[at])
        for at, (source, target) in enumerate(sources)
    ]
    for copy in copies:
        copy.start()
    ordering = token_order(sizes, tokens)
    order = jnp.where(ordering, 1.0, 0.0).astype(bf16)
    ny, nz, nc = sizes
    device = (lax.axis_index("y") * nz + lax.axis_index("z")) * nc + lax.axis_index("c")
    for copy in copies[0:3]:
        copy.wait()
    ordered = jnp.dot(order, hidden_ref[...], preferred_element_type=f32).astype(bf16)
    place = column_of(ordering, (targets_ref[...] - device * (parts * columns)).astype(f32))
    place_ref[...] = jnp.broadcast_to(place, place_ref.shape)
    mine = lax.broadcasted_iota(i32, (pair, tokens), 1) == (
        device * pair + lax.broadcasted_iota(i32, (pair, tokens), 0)
    )
    own_scale_ref[...] = jnp.broadcast_to(column_of(mine, scale_ref[...]), own_scale_ref.shape)
    for part in range(parts):
        copies[3 + part].wait()
        coded_logits(ordered, part_ref[part], out_ref.at[part])

    @pl.when(lax.axis_index("c") == 0)
    def _():
        target_rows(weight_hbm, place_ref, hard_ref, weight_ref, weight_sems)


def exp_kernel(codes_ref, place_ref, out_ref):
    parts, rows, columns = codes_ref.shape
    tokens = rows - SIDE
    raw = None
    for part in range(parts):
        exponent = to_f32(codes_ref[part, tokens:, :])[0:1]
        term = to_f32(codes_ref[part, 0:tokens, :]) * jnp.exp2(exponent)
        raw = term if raw is None else raw + term
    tangent = jnp.tanh(raw / logit_cap)
    exp_terms = jnp.exp(logit_cap * tangent)
    slope = 1.0 - tangent * tangent
    sums = jnp.sum(exp_terms, axis=1, keepdims=True)
    targets = place_ref[:, 0:1]
    places = lax.broadcasted_iota(i32, raw.shape, 1) + lax.axis_index("w") * columns
    at_target = jnp.sum(
        jnp.where(targets == places.astype(f32), slope, 0.0), axis=1, keepdims=True
    )
    diagonal = eye(tokens)
    sum_row = jnp.sum(jnp.where(diagonal, sums, 0.0), axis=0, keepdims=True)
    target_row = jnp.sum(jnp.where(diagonal, at_target, 0.0), axis=0, keepdims=True)
    which = lax.broadcasted_iota(i32, (SIDE, tokens), 0)
    side = jnp.where(which == 0, sum_row, jnp.where(which == 1, target_row, 0.0))
    high = side.astype(bf16)
    low = (side - high.astype(f32)).astype(bf16)
    pieces = [high, low]
    if columns > 2 * tokens:
        pieces.append(jnp.zeros((SIDE, columns - 2 * tokens), bf16))
    grads = (exp_terms * slope).astype(bf16)
    side = jnp.concatenate(pieces, axis=1)
    for part in range(out_ref.shape[0]):
        out_ref[part, 0:tokens, :] = grads
        out_ref[part, tokens:, :] = side


def target_rows(weight_hbm, place_ref, rows_ref, weight_ref, sems):
    tokens = rows_ref.shape[0]
    blocks = sems.shape[0]
    columns = weight_ref.shape[0] // blocks
    copies = []
    for at in range(blocks):
        block = pl.ds(at * columns, columns)
        copies.append(
            pltpu.make_async_copy(weight_hbm.at[block], weight_ref.at[block], sems.at[at])
        )
        copies[-1].start()
    targets = place_ref[:, 0:1]
    lane = lax.broadcasted_iota(i32, (tokens, columns), 1)
    total = None
    for at in range(blocks):
        at_target = targets == (lane + at * columns).astype(f32)
        at_target = jnp.where(at_target, 1.0, 0.0).astype(bf16)
        copies[at].wait()
        weight = weight_ref[pl.ds(at * columns, columns)]
        term = jnp.dot(at_target, weight, preferred_element_type=f32)
        total = term if total is None else total + term
    rows_ref[...] = total.astype(bf16)


def hidden_kernel(
    grads_ref, weight_hbm, place_ref, hard_ref, weight_ref, mine_ref, other_ref,
    late_hard_ref, late_weight_ref, sum_ref, sems,
):
    @pl.when(lax.axis_index("c") == 0)
    def _():
        hidden_work(grads_ref, weight_ref, hard_ref, mine_ref, other_ref, sum_ref)

    @pl.when(lax.axis_index("c") == 1)
    def _():
        target_rows(weight_hbm, place_ref, late_hard_ref, late_weight_ref, sems)
        hidden_work(grads_ref, late_weight_ref, late_hard_ref, mine_ref, other_ref, sum_ref)


def hidden_work(grads_ref, weight_ref, hard_ref, mine_ref, other_ref, sum_ref):
    parts, rows, columns = grads_ref.shape
    tokens, width = rows - SIDE, weight_ref.shape[1]
    own = mine_ref.shape[0]
    side = None
    for part in range(parts):
        term = grads_ref[part, tokens:, :].astype(f32)
        term = term[:, 0:tokens] + term[:, tokens : 2 * tokens]
        side = term if side is None else side + term
    diagonal = eye(tokens)
    sums = column_of(diagonal, side[0:1, :])
    slope = column_of(diagonal, side[1:2, :])
    sum_ref[:, width : 2 * width] = hard_ref[...].astype(f32) * slope
    sum_ref[:, 2 * width :] = jnp.broadcast_to(sums, (tokens, LANES))
    soft = None
    for part in range(parts):
        weight = weight_ref[pl.ds(part * columns, columns)]
        term = jnp.dot(grads_ref[part, 0:tokens, :], weight, preferred_element_type=f32)
        soft = term if soft is None else soft + term
    sum_ref[:, 0:width] = soft
    core = lax.axis_index("c")
    mine_ref[...] = sum_ref[rows_of(core, own)]
    theirs = sum_ref[rows_of(1 - core, own)]
    store_rows(other_ref, theirs[:, 0:width], theirs[:, width : 2 * width], theirs[:, 2 * width : 2 * width + 1])


def scalar_codes(values):
    exponent = jnp.floor(jnp.log2(jnp.maximum(values, 1e-30))) - 24.0
    scaled = values * jnp.exp2(-exponent)
    high = jnp.floor(scaled * (1.0 / 4096.0))
    return [exponent, high, scaled - high * 4096.0]


def scalar_of(side, at):
    return (side[:, at + 1 : at + 2] * 4096.0 + side[:, at + 2 : at + 3]) * jnp.exp2(
        side[:, at : at + 1]
    )


def in_lanes(columns):
    lane = lax.broadcasted_iota(i32, (columns[0].shape[0], LANES), 1)
    side = jnp.zeros(lane.shape, f32)
    for at, value in enumerate(columns):
        side = jnp.where(lane == at, value, side)
    return side.astype(i32).astype(i16)


def row_exponent(values):
    return exponent_of(jnp.max(jnp.abs(values), axis=1, keepdims=True))


def store_rows(out_ref, soft, hard, total):
    soft_exp, hard_exp = row_exponent(soft), row_exponent(hard)
    pieces = (
        code(soft, soft_exp),
        code(hard, hard_exp),
        in_lanes([soft_exp, hard_exp, *scalar_codes(total)]),
    )
    parts, rows, _ = out_ref.shape
    at = 0
    for piece in pieces:
        for part in range(parts):
            out_ref[part, :, at : at + piece.shape[1]] = piece[part * rows : (part + 1) * rows]
        at += piece.shape[1]


def decoded_sum(width, in_ref):
    sums = None
    for part in range(in_ref.shape[0]):
        side = to_f32(in_ref[part, :, 2 * width :])
        terms = (
            to_f32(in_ref[part, :, 0:width]) * jnp.exp2(side[:, 0:1]),
            to_f32(in_ref[part, :, width : 2 * width]) * jnp.exp2(side[:, 1:2]),
            scalar_of(side, 2),
        )
        sums = terms if sums is None else tuple(a + b for a, b in zip(sums, terms))
    return sums


def cores_kernel(width, mine_ref, other_ref, out_ref):
    soft, hard, total = decoded_sum(width, other_ref)
    soft = soft + mine_ref[:, 0:width]
    hard = hard + mine_ref[:, width : 2 * width]
    store_rows(out_ref, soft, hard, total + mine_ref[:, 2 * width : 2 * width + 1])


def y_kernel(width, in_ref, out_ref):
    store_rows(out_ref, *decoded_sum(width, in_ref))


def z_kernel(width, in_ref, scale_ref, out_ref):
    soft, hard, total = decoded_sum(width, in_ref)
    scale = scale_ref[:, 0:1]
    weighting = scale * (1.0 + 2.0 * zloss_weight * jnp.log(total))
    out_ref[...] = (weighting / total * soft - scale * hard).astype(bf16)


def params():
    return pltpu.CompilerParams(vmem_limit_bytes=VMEM_BYTES)


def on_device(sizes, hidden, head_weight, targets, token_scale):
    ny, nz, nc = sizes
    nw = lax.axis_size("w")
    tokens, width = hidden.shape
    vocab = head_weight.shape[0]
    columns = vocab // nw
    rows = tokens + SIDE
    pair = tokens // (ny * nz * nc)
    lanes = 2 * width + LANES
    hbm = pl.BlockSpec(memory_space=pltpu.HBM)
    vmem = pl.BlockSpec(memory_space=pltpu.VMEM)

    def shape(*dims, dtype=f32):
        return jax.ShapeDtypeStruct(dims, dtype)

    def swap(x):
        return lax.ppermute(x, "c", [(0, 1), (1, 0)])

    in_hbm = functools.partial(pltpu.with_memory_space_constraint, memory_space=pltpu.HBM)
    weight_hbm = in_hbm(head_weight)
    hard_shapes = [shape(tokens, width, dtype=bf16), shape(vocab, width, dtype=bf16)]
    codes, place, scale, *hard = pl.pallas_call(
        functools.partial(logits_kernel, sizes),
        in_specs=[hbm] * 4,
        out_specs=[vmem] * 5,
        out_shape=[
            shape(nw, rows, columns, dtype=i16),
            shape(tokens, LANES),
            shape(pair, LANES),
            *hard_shapes,
        ],
        scratch_shapes=[
            pltpu.VMEM((tokens, width), bf16),
            pltpu.VMEM((nw, columns, width), bf16),
            pltpu.VMEM((1, tokens), i32),
            pltpu.VMEM((1, tokens), f32),
            pltpu.SemaphoreType.DMA((nw + 3,)),
            pltpu.SemaphoreType.DMA((nw,)),
        ],
        compiler_params=params(),
        name="logits",
    )(
        in_hbm(hidden),
        weight_hbm,
        in_hbm(targets.reshape(1, tokens)),
        in_hbm(token_scale.reshape(1, tokens)),
    )
    codes = lax.all_to_all(codes, "w", 0, 0, tiled=True)
    grads = pl.pallas_call(
        exp_kernel,
        out_shape=shape(nw, rows, columns, dtype=bf16),
        compiler_params=params(),
        name="exponentials",
    )(codes, place)
    grads = lax.all_to_all(grads, "w", 0, 0, tiled=True)
    mine, other = pl.pallas_call(
        hidden_kernel,
        in_specs=[vmem, hbm] + [vmem] * 3,
        out_specs=[vmem] * 2,
        out_shape=[shape(tokens // nc, lanes), shape(1, tokens // nc, lanes, dtype=i16)],
        scratch_shapes=[
            pltpu.VMEM((tokens, width), bf16),
            pltpu.VMEM((vocab, width), bf16),
            pltpu.VMEM((tokens, lanes), f32),
            pltpu.SemaphoreType.DMA((nw,)),
        ],
        compiler_params=params(),
        name="hidden_partial",
    )(grads, weight_hbm, place, *hard)
    other = swap(other)
    sums = pl.pallas_call(
        functools.partial(cores_kernel, width),
        out_shape=shape(ny, nz * pair, lanes, dtype=i16),
        compiler_params=params(),
        name="sum_cores",
    )(mine, other)
    sums = lax.all_to_all(sums, "y", 0, 0, tiled=True)
    sums = pl.pallas_call(
        functools.partial(y_kernel, width),
        out_shape=shape(nz, pair, lanes, dtype=i16),
        compiler_params=params(),
        name="sum_y",
    )(sums)
    sums = lax.all_to_all(sums, "z", 0, 0, tiled=True)
    return pl.pallas_call(
        functools.partial(z_kernel, width),
        out_shape=shape(pair, width, dtype=bf16),
        compiler_params=params(),
        name="sum_z",
    )(sums, scale)


def solution(mesh):
    vocab, width = mesh.devices.shape
    sizes = (4, vocab // 8, 2)
    inner = Mesh(mesh.devices.reshape(*sizes, width), ("y", "z", "c", "w"))
    vocab_axes = ("y", "z", "c")
    placed = (P(None, "w"), P(vocab_axes, "w"), P(), P())
    return jax.shard_map(
        functools.partial(on_device, sizes),
        mesh=inner,
        in_specs=placed,
        out_specs=P(vocab_axes, "w"),
        check_vma=False,
    )
```

time: 106 us -> 90.5 us (0.85)
  blocking collectives: 38.2 us -> 73.9 us
  waiting for transfers between devices: 29.6 us -> 2.02 us
  starting transfers between devices: 19.7 us -> 1.92 us
  local copies, waits for them, and re-layouts: 6.77 us -> 0 us
  Pallas kernels: 10 us -> 12.3 us
  other arithmetic: 1.24 us -> 0 us
    all_to_all x1 -> x2, blocking collectives: 5.73 us -> 45.2 us  [the longest x1 28.8 us: on_device(): sums = lax.all_to_all(sums, 'z', 0, 0, tiled=True)]
    all_to_all x2 -> x0, waiting for transfers between devices: 29.6 us -> none  [the longest x1 15.8 us: on_device(): codes = lax.all_to_all(codes, 'w', 0, 0, tiled=True)]
    all_to_all x2 -> x0, starting transfers between devices: 19.7 us -> none  [the longest x1 15.3 us: on_device(): sums = lax.all_to_all(sums.reshape(nz, pair, lanes), 'z', 0, 0, tiled=True)]
    unnamed x10 -> x0, local copies, waits for them, and re-layouts: 5.74 us -> none
    all_to_all x1, blocking collectives: 17.3 us -> 13.6 us  [on_device(): grads = lax.all_to_all(grads, 'w', 0, 0, tiled=True)]
    pallas_call x5 -> x6, Pallas kernels: 10 us -> 12.3 us  [the longest x1 7.8 us: on_device(): pl.pallas_call(functools.partial(logits_kernel, sizes), in_specs=[hbm] *...]
    ppermute x0 -> x1, waiting for transfers between devices: none -> 2.02 us  [swap(): return lax.ppermute(x, 'c', [(0, 1), (1, 0)])]
    ppermute x0 -> x1, starting transfers between devices: none -> 1.92 us  [swap(): return lax.ppermute(x, 'c', [(0, 1), (1, 0)])]
  transfers between devices with their start and end apart: 2 -> 1, of which waited for: 2 -> 1; matrix products, arithmetic and copies ran while one was open for 0% -> 0% of each run, Pallas kernels for 0% -> 0%
where the time goes in v3:
time: 90.5 us; the launch traced here: 90.3 us
  blocking collectives  73.9 us (82%)
  Pallas kernels  12.3 us (14%)
  waiting for transfers between devices  2.02 us (2%)
  starting transfers between devices  1.92 us (2%)
    all_to_all x1, blocking collectives, on_device(): sums = lax.all_to_all(sums, 'z', 0, 0, tiled=True)  28.8 us
    all_to_all x1, blocking collectives, on_device(): codes = lax.all_to_all(codes, 'w', 0, 0, tiled=True)  16.4 us
    all_to_all x1, blocking collectives, on_device(): sums = lax.all_to_all(sums, 'y', 0, 0, tiled=True)  15.1 us
    all_to_all x1, blocking collectives, on_device(): grads = lax.all_to_all(grads, 'w', 0, 0, tiled=True)  13.6 us
    pallas_call x1, Pallas kernels, on_device(): pl.pallas_call(functools.partial(logits_kernel, sizes), in_specs=[hbm] *...  7.8 us
    pallas_call x1, Pallas kernels, on_device(): pl.pallas_call(hidden_kernel, in_specs=[vmem, hbm] + [vmem] * 3, out_spec...  2.15 us
    ppermute x1, waiting for transfers between devices, swap(): return lax.ppermute(x, 'c', [(0, 1), (1, 0)])  2.02 us
    ppermute x1, starting transfers between devices, swap(): return lax.ppermute(x, 'c', [(0, 1), (1, 0)])  1.92 us
  transfers between devices with their start and end apart: 1, of which 1 were waited for; matrix products, arithmetic and copies ran while one was open for 0% of the time, Pallas kernels for 0%

profile of v3, /device:TPU:32, one launch (start us, length us, event | category | flops | bytes accessed | tf_op | source)
XLA Modules:
  0.0 90.3 jit_solution(17219403872780779395)
XLA Ops:
  0.0 7.8 %logits.1 = (s16[4,272,512]{2,1,0:T(8,128)(2,1)S(1)}, f32[256,128]{1,0:T(8,128)S(1)}, f32[2,128]{1,0:T(2,128)S(1)}, bf16[256,1152]{1,0:T(8,128)(2,1)S(1)}, bf16[2048,1152]{1,0:T(8,128)(2,1)S(1)}) custom-call(bf16[256,1152]{1,0:T(8,128)(2,1)} %hidden_hbm.1, bf16[2048,1152]{1,0:T(8,128)(2,1)} %weight_hbm.3, s32[1,256]{1,0:T(1,128)} %bitcast.2, f32[1,256]{1,0:T(1,128)} %bitcast.3), custom_call_target="tpu_custom_call" | custom-call | tf_op jit(solution)/shard_map/logits/pallas_call | solution.py:301
  7.8 16.4 %all_to_all.20.codes_ref = s16[4,272,512]{2,1,0:T(8,128)(2,1)S(1)} all-to-all(s16[4,272,512]{2,1,0:T(8,128)(2,1)S(1)} %get-tuple-element.12), channel_id=1, replica_groups=mesh['y'=4,'z'=16,'c'=2,'w'=4] {'w'}, dimensions={0} | all-to-all | bytes 2228224 | tf_op jit(solution)/shard_map/all_to_all | solution.py:327
  24.2 0.7 exponentials.1
  24.9 13.6 %all_to_all.21.grads_ref = bf16[4,272,512]{2,1,0:T(8,128)(2,1)S(1)} all-to-all(bf16[4,272,512]{2,1,0:T(8,128)(2,1)S(1)} %exponentials.1), channel_id=1, replica_groups=mesh['y'=4,'z'=16,'c'=2,'w'=4] {'w'}, dimensions={0} | all-to-all | bytes 2228224 | tf_op jit(solution)/shard_map/all_to_all | solution.py:334
  38.5 2.2 %hidden_partial.1 = (f32[128,2432]{1,0:T(8,128)S(1)}, s16[1,128,2432]{2,1,0:T(8,128)(2,1)S(1)}) custom-call(bf16[4,272,512]{2,1,0:T(8,128)(2,1)S(1)} %all_to_all.21.grads_ref, bf16[2048,1152]{1,0:T(8,128)(2,1)} %weight_hbm.3, f32[256,128]{1,0:T(8,128)S(1)} %get-tuple-element.13.place_ref, bf16[256,1152]{1,0:T(8,128)(2,1)S(1)} %get-tuple-element.14.hard_ref, ...), custom_call_target="tpu_custom_call" | custom-call | tf_op jit(solution)/shard_map/hidden_partial/pallas_call | solution.py:335
  40.7 1.9 %collective-permute-start = (s16[1,128,2432]{2,1,0:T(8,128)(2,1)S(1)}, s16[1,128,2432]{2,1,0:T(8,128)(2,1)S(1)}, u32[]{:S(2)}, u32[]{:S(2)}) collective-permute-start(s16[1,128,2432]{2,1,0:T(8,128)(2,1)S(1)} %get-tuple-element.17), channel_id=1, source_target_pairs={{0,4},{4,0},{1,5},{5,1},{2,6},{6,2},{3,7},{7,3},{8,12},{12,8},{9,1... | collective-permute-start | bytes 1867784 | tf_op jit(solution)/shard_map/ppermute | solution.py:296
  42.6 2.0 %collective-permute-done.other_ref = s16[1,128,2432]{2,1,0:T(8,128)(2,1)S(1)} collective-permute-done((s16[1,128,2432]{2,1,0:T(8,128)(2,1)S(1)}, s16[1,128,2432]{2,1,0:T(8,128)(2,1)S(1)}, u32[]{:S(2)}, u32[]{:S(2)}) %collective-permute-start) | collective-permute-done | bytes 622624 | tf_op jit(solution)/shard_map/ppermute | solution.py:296
  44.6 0.6 sum_cores.1
  45.2 15.1 %all_to_all.22.in_ref = s16[4,32,2432]{2,1,0:T(8,128)(2,1)S(1)} all-to-all(s16[4,32,2432]{2,1,0:T(8,128)(2,1)S(1)} %sum_cores.1), channel_id=1, replica_groups=mesh['y'=4,'z'=16,'c'=2,'w'=4] {'y'}, dimensions={0} | all-to-all | bytes 1245184 | tf_op jit(solution)/shard_map/all_to_all | solution.py:356
  60.3 0.3 sum_y.1
  60.6 28.8 %all_to_all.23.in_ref = s16[16,2,2432]{2,1,0:T(2,128)(2,1)S(1)} all-to-all(s16[16,2,2432]{2,1,0:T(2,128)(2,1)S(1)} %sum_y.1), channel_id=1, replica_groups=mesh['y'=4,'z'=16,'c'=2,'w'=4] {'z'}, dimensions={0} | all-to-all | bytes 311296 | tf_op jit(solution)/shard_map/all_to_all | solution.py:363
  89.4 0.9 sum_z.1
Async XLA Ops:
  40.7 3.9 %collective-permute-start = (s16[1,128,2432]{2,1,0:T(8,128)(2,1)S(1)}, s16[1,128,2432]{2,1,0:T(8,128)(2,1)S(1)}, u32[]{:S(2)}, u32[]{:S(2)}) collective-permute-start(s16[1,128,2432]{2,1,0:T(8,128)(2,1)S(1)} %get-tuple-element.17), channel_id=1, source_target_pairs={{0,4},{4,0},{1,5},{5,1},{2,6},{6,2},{3,7},{7,3},{8,12},{12,8},{9,1... | collective-permute-start | bytes 1867784 | tf_op jit(solution)/shard_map/ppermute | solution.py:296

commit v4 on v3

--- a/solution.py
+++ b/solution.py
@@ -53,11 +53,8 @@
     return pl.ds(pl.multiple_of(part * columns, columns), columns)
 
 
-def coded_logits(ordered, weight, out_ref):
-    tokens = ordered.shape[0]
-    partial = lax.dot_general(
-        ordered, weight, (((1,), (1,)), ((), ())), preferred_element_type=f32
-    )
+def store_coded(partial, out_ref):
+    tokens = partial.shape[0]
     exponent = exponent_of(jnp.max(jnp.abs(partial), axis=0, keepdims=True))
     out_ref[0:tokens, :] = code(partial, exponent)
     out_ref[tokens:, :] = jnp.broadcast_to(
@@ -86,18 +83,26 @@
     order = jnp.where(ordering, 1.0, 0.0).astype(bf16)
     ny, nz, nc = sizes
     device = (lax.axis_index("y") * nz + lax.axis_index("z")) * nc + lax.axis_index("c")
-    for copy in copies[0:3]:
+    copies[0].wait()
+    ordered = jnp.dot(order, hidden_ref[...], preferred_element_type=f32).astype(bf16)
+    for copy in copies[1:3]:
         copy.wait()
-    ordered = jnp.dot(order, hidden_ref[...], preferred_element_type=f32).astype(bf16)
     place = column_of(ordering, (targets_ref[...] - device * (parts * columns)).astype(f32))
     place_ref[...] = jnp.broadcast_to(place, place_ref.shape)
     mine = lax.broadcasted_iota(i32, (pair, tokens), 1) == (
         device * pair + lax.broadcasted_iota(i32, (pair, tokens), 0)
     )
     own_scale_ref[...] = jnp.broadcast_to(column_of(mine, scale_ref[...]), own_scale_ref.shape)
+    last = None
     for part in range(parts):
         copies[3 + part].wait()
-        coded_logits(ordered, part_ref[part], out_ref.at[part])
+        partial = lax.dot_general(
+            ordered, part_ref[part], (((1,), (1,)), ((), ())), preferred_element_type=f32
+        )
+        if last is not None:
+            store_coded(last, out_ref.at[part - 1])
+        last = partial
+    store_coded(last, out_ref.at[parts - 1])
 
     @pl.when(lax.axis_index("c") == 0)
     def _():
@@ -162,44 +167,61 @@
     rows_ref[...] = total.astype(bf16)
 
 
-def hidden_kernel(
-    grads_ref, weight_hbm, place_ref, hard_ref, weight_ref, mine_ref, other_ref,
-    late_hard_ref, late_weight_ref, sum_ref, sems,
-):
-    @pl.when(lax.axis_index("c") == 0)
-    def _():
-        hidden_work(grads_ref, weight_ref, hard_ref, mine_ref, other_ref, sum_ref)
-
-    @pl.when(lax.axis_index("c") == 1)
-    def _():
-        target_rows(weight_hbm, place_ref, late_hard_ref, late_weight_ref, sems)
-        hidden_work(grads_ref, late_weight_ref, late_hard_ref, mine_ref, other_ref, sum_ref)
-
-
-def hidden_work(grads_ref, weight_ref, hard_ref, mine_ref, other_ref, sum_ref):
+def hidden_rows(which, own, grads_ref, weight_ref, hard_ref):
     parts, rows, columns = grads_ref.shape
-    tokens, width = rows - SIDE, weight_ref.shape[1]
-    own = mine_ref.shape[0]
+    tokens = rows - SIDE
+    mine = pl.ds(which * own, own)
     side = None
     for part in range(parts):
         term = grads_ref[part, tokens:, :].astype(f32)
         term = term[:, 0:tokens] + term[:, tokens : 2 * tokens]
         side = term if side is None else side + term
-    diagonal = eye(tokens)
-    sums = column_of(diagonal, side[0:1, :])
-    slope = column_of(diagonal, side[1:2, :])
-    sum_ref[:, width : 2 * width] = hard_ref[...].astype(f32) * slope
-    sum_ref[:, 2 * width :] = jnp.broadcast_to(sums, (tokens, LANES))
+    token = lax.broadcasted_iota(i32, (own, tokens), 1)
+    mask = token == lax.broadcasted_iota(i32, (own, tokens), 0) + which * own
+    sums = column_of(mask, side[0:1, :])
+    slope = column_of(mask, side[1:2, :])
     soft = None
     for part in range(parts):
         weight = weight_ref[pl.ds(part * columns, columns)]
-        term = jnp.dot(grads_ref[part, 0:tokens, :], weight, preferred_element_type=f32)
+        term = jnp.dot(grads_ref[part, mine, :], weight, preferred_element_type=f32)
         soft = term if soft is None else soft + term
-    sum_ref[:, 0:width] = soft
-    core = lax.axis_index("c")
-    mine_ref[...] = sum_ref[rows_of(core, own)]
-    theirs = sum_ref[rows_of(1 - core, own)]
-    store_rows(other_ref, theirs[:, 0:width], theirs[:, width : 2 * width], theirs[:, 2 * width : 2 * width + 1])
+    return soft, hard_ref[mine].astype(f32) * slope, sums
+
+
+def other_hidden_kernel(
+    grads_ref, weight_hbm, place_ref, hard_ref, weight_ref,
+    other_ref, late_hard_ref, late_weight_ref, sems,
+):
+    own = other_ref.shape[1]
+
+    @pl.when(lax.axis_index("c") == 0)
+    def _():
+        store_rows(other_ref, *hidden_rows(1, own, grads_ref, weight_ref, hard_ref))
+
+    @pl.when(lax.axis_index("c") == 1)
+    def _():
+        target_rows(weight_hbm, place_ref, late_hard_ref, late_weight_ref, sems)
+        store_rows(other_ref, *hidden_rows(0, own, grads_ref, late_weight_ref, late_hard_ref))
+
+
+def own_hidden_kernel(
+    grads_ref, hard_ref, weight_ref, late_hard_ref, late_weight_ref, out_ref
+):
+    own = out_ref.shape[0]
+    width = weight_ref.shape[1]
+
+    def store(soft, hard, sums):
+        out_ref[:, 0:width] = soft
+        out_ref[:, width : 2 * width] = hard
+        out_ref[:, 2 * width :] = jnp.broadcast_to(sums, (own, LANES))
+
+    @pl.when(lax.axis_index("c") == 0)
+    def _():
+        store(*hidden_rows(0, own, grads_ref, weight_ref, hard_ref))
+
+    @pl.when(lax.axis_index("c") == 1)
+    def _():
+        store(*hidden_rows(1, own, grads_ref, late_weight_ref, late_hard_ref))
 
 
 def scalar_codes(values):
@@ -332,21 +354,22 @@
         name="exponentials",
     )(codes, place)
     grads = lax.all_to_all(grads, "w", 0, 0, tiled=True)
-    mine, other = pl.pallas_call(
-        hidden_kernel,
+    other, *late_hard = pl.pallas_call(
+        other_hidden_kernel,
         in_specs=[vmem, hbm] + [vmem] * 3,
-        out_specs=[vmem] * 2,
-        out_shape=[shape(tokens // nc, lanes), shape(1, tokens // nc, lanes, dtype=i16)],
-        scratch_shapes=[
-            pltpu.VMEM((tokens, width), bf16),
-            pltpu.VMEM((vocab, width), bf16),
-            pltpu.VMEM((tokens, lanes), f32),
-            pltpu.SemaphoreType.DMA((nw,)),
-        ],
-        compiler_params=params(),
-        name="hidden_partial",
+        out_specs=[vmem] * 3,
+        out_shape=[shape(1, tokens // nc, lanes, dtype=i16), *hard_shapes],
+        scratch_shapes=[pltpu.SemaphoreType.DMA((nw,))],
+        compiler_params=params(),
+        name="other_hidden",
     )(grads, weight_hbm, place, *hard)
     other = swap(other)
+    mine = pl.pallas_call(
+        own_hidden_kernel,
+        out_shape=shape(tokens // nc, lanes),
+        compiler_params=params(),
+        name="own_hidden",
+    )(grads, *hard, *late_hard)
     sums = pl.pallas_call(
         functools.partial(cores_kernel, width),
         out_shape=shape(ny, nz * pair, lanes, dtype=i16),

time: 90.5 us -> 89.5 us (0.989)
    pallas_call x1 -> x2, Pallas kernels: 2.15 us -> 2.15 us  [the longest x1 1.27 us: on_device(): pl.pallas_call(other_hidden_kernel, in_specs=[vmem, hbm] + [vmem] * 3, ou...]
  transfers between devices with their start and end apart: 1 -> 1, of which waited for: 1 -> 1; matrix products, arithmetic and copies ran while one was open for 0% -> 0% of each run, Pallas kernels for 0% -> 1%
where the time goes in v4:
time: 89.5 us; the launch traced here: 89.2 us
  blocking collectives  73.9 us (83%)
  Pallas kernels  12.2 us (14%)
  starting transfers between devices  1.92 us (2%)
  waiting for transfers between devices  1.13 us (1%)
    all_to_all x1, blocking collectives, on_device(): sums = lax.all_to_all(sums, 'z', 0, 0, tiled=True)  28.8 us
    all_to_all x1, blocking collectives, on_device(): codes = lax.all_to_all(codes, 'w', 0, 0, tiled=True)  16.4 us
    all_to_all x1, blocking collectives, on_device(): sums = lax.all_to_all(sums, 'y', 0, 0, tiled=True)  15.1 us
    all_to_all x1, blocking collectives, on_device(): grads = lax.all_to_all(grads, 'w', 0, 0, tiled=True)  13.6 us
    pallas_call x1, Pallas kernels, on_device(): pl.pallas_call(functools.partial(logits_kernel, sizes), in_specs=[hbm] *...  7.64 us
    ppermute x1, starting transfers between devices, swap(): return lax.ppermute(x, 'c', [(0, 1), (1, 0)])  1.92 us
  transfers between devices with their start and end apart: 1, of which 1 were waited for; matrix products, arithmetic and copies ran while one was open for 0% of the time, Pallas kernels for 1%

profile of v4, /device:TPU:32, one launch (start us, length us, event | category | flops | bytes accessed | tf_op | source)
XLA Modules:
  0.0 89.2 jit_solution(7745130584084474609)
XLA Ops:
  0.0 7.6 %logits.1 = (s16[4,272,512]{2,1,0:T(8,128)(2,1)S(1)}, f32[256,128]{1,0:T(8,128)S(1)}, f32[2,128]{1,0:T(2,128)S(1)}, bf16[256,1152]{1,0:T(8,128)(2,1)S(1)}, bf16[2048,1152]{1,0:T(8,128)(2,1)S(1)}) custom-call(bf16[256,1152]{1,0:T(8,128)(2,1)} %hidden_hbm.1, bf16[2048,1152]{1,0:T(8,128)(2,1)} %weight_hbm.3, s32[1,256]{1,0:T(1,128)} %bitcast.2, f32[1,256]{1,0:T(1,128)} %bitcast.3), custom_call_target="tpu_custom_call" | custom-call | tf_op jit(solution)/shard_map/logits/pallas_call | solution.py:323
  7.6 16.4 %all_to_all.20.codes_ref = s16[4,272,512]{2,1,0:T(8,128)(2,1)S(1)} all-to-all(s16[4,272,512]{2,1,0:T(8,128)(2,1)S(1)} %get-tuple-element.13), channel_id=1, replica_groups=mesh['y'=4,'z'=16,'c'=2,'w'=4] {'w'}, dimensions={0} | all-to-all | bytes 2228224 | tf_op jit(solution)/shard_map/all_to_all | solution.py:349
  24.0 0.7 exponentials.1
  24.7 13.6 %all_to_all.21.grads_ref = bf16[4,272,512]{2,1,0:T(8,128)(2,1)S(1)} all-to-all(bf16[4,272,512]{2,1,0:T(8,128)(2,1)S(1)} %exponentials.1), channel_id=1, replica_groups=mesh['y'=4,'z'=16,'c'=2,'w'=4] {'w'}, dimensions={0} | all-to-all | bytes 2228224 | tf_op jit(solution)/shard_map/all_to_all | solution.py:356
  38.3 1.3 %other_hidden.1 = (s16[1,128,2432]{2,1,0:T(8,128)(2,1)S(1)}, bf16[256,1152]{1,0:T(8,128)(2,1)S(1)}, bf16[2048,1152]{1,0:T(8,128)(2,1)S(1)}) custom-call(bf16[4,272,512]{2,1,0:T(8,128)(2,1)S(1)} %all_to_all.21.grads_ref, bf16[2048,1152]{1,0:T(8,128)(2,1)} %weight_hbm.3, f32[256,128]{1,0:T(8,128)S(1)} %get-tuple-element.14.place_ref, ...), custom_call_target="tpu_custom_call" | custom-call | tf_op jit(solution)/shard_map/other_hidden/pallas_call | solution.py:357
  39.6 1.9 %collective-permute-start = (s16[1,128,2432]{2,1,0:T(8,128)(2,1)S(1)}, s16[1,128,2432]{2,1,0:T(8,128)(2,1)S(1)}, u32[]{:S(2)}, u32[]{:S(2)}) collective-permute-start(s16[1,128,2432]{2,1,0:T(8,128)(2,1)S(1)} %get-tuple-element.19), channel_id=1, source_target_pairs={{0,4},{4,0},{1,5},{5,1},{2,6},{6,2},{3,7},{7,3},{8,12},{12,8},{9,1... | collective-permute-start | bytes 1867784 | tf_op jit(solution)/shard_map/ppermute | solution.py:318
  41.6 0.9 own_hidden.1.mine_ref
  42.4 1.1 %collective-permute-done.other_ref = s16[1,128,2432]{2,1,0:T(8,128)(2,1)S(1)} collective-permute-done((s16[1,128,2432]{2,1,0:T(8,128)(2,1)S(1)}, s16[1,128,2432]{2,1,0:T(8,128)(2,1)S(1)}, u32[]{:S(2)}, u32[]{:S(2)}) %collective-permute-start) | collective-permute-done | bytes 622624 | tf_op jit(solution)/shard_map/ppermute | solution.py:318
  43.6 0.6 sum_cores.1
  44.1 15.1 %all_to_all.22.in_ref = s16[4,32,2432]{2,1,0:T(8,128)(2,1)S(1)} all-to-all(s16[4,32,2432]{2,1,0:T(8,128)(2,1)S(1)} %sum_cores.1), channel_id=1, replica_groups=mesh['y'=4,'z'=16,'c'=2,'w'=4] {'y'}, dimensions={0} | all-to-all | bytes 1245184 | tf_op jit(solution)/shard_map/all_to_all | solution.py:379
  59.2 0.3 sum_y.1
  59.6 28.8 %all_to_all.23.in_ref = s16[16,2,2432]{2,1,0:T(2,128)(2,1)S(1)} all-to-all(s16[16,2,2432]{2,1,0:T(2,128)(2,1)S(1)} %sum_y.1), channel_id=1, replica_groups=mesh['y'=4,'z'=16,'c'=2,'w'=4] {'z'}, dimensions={0} | all-to-all | bytes 311296 | tf_op jit(solution)/shard_map/all_to_all | solution.py:386
  88.4 0.9 sum_z.1
Async XLA Ops:
  39.6 3.9 %collective-permute-start = (s16[1,128,2432]{2,1,0:T(8,128)(2,1)S(1)}, s16[1,128,2432]{2,1,0:T(8,128)(2,1)S(1)}, u32[]{:S(2)}, u32[]{:S(2)}) collective-permute-start(s16[1,128,2432]{2,1,0:T(8,128)(2,1)S(1)} %get-tuple-element.19), channel_id=1, source_target_pairs={{0,4},{4,0},{1,5},{5,1},{2,6},{6,2},{3,7},{7,3},{8,12},{12,8},{9,1... | collective-permute-start | bytes 1867784 | tf_op jit(solution)/shard_map/ppermute | solution.py:318

commit v5 on v4

--- a/solution.py
+++ b/solution.py
@@ -289,7 +289,17 @@
 
 
 def z_kernel(width, in_ref, scale_ref, out_ref):
-    soft, hard, total = decoded_sum(width, in_ref)
+    rows, pair = in_ref.shape[0], out_ref.shape[0]
+    side = to_f32(in_ref[:, 2 * width :])
+    sums = (
+        to_f32(in_ref[:, 0:width]) * jnp.exp2(side[:, 0:1]),
+        to_f32(in_ref[:, width : 2 * width]) * jnp.exp2(side[:, 1:2]),
+        scalar_of(side, 2),
+    )
+    while rows > pair:
+        rows //= 2
+        sums = tuple(x[0:rows] + x[rows:] for x in sums)
+    soft, hard, total = sums
     scale = scale_ref[:, 0:1]
     weighting = scale * (1.0 + 2.0 * zloss_weight * jnp.log(total))
     out_ref[...] = (weighting / total * soft - scale * hard).astype(bf16)
@@ -389,7 +399,7 @@
         out_shape=shape(pair, width, dtype=bf16),
         compiler_params=params(),
         name="sum_z",
-    )(sums, scale)
+    )(sums.reshape(nz * pair, lanes), scale)
 
 
 def solution(mesh):

time: 89.5 us -> 89.5 us (level)
  no operation moved by 1% of the time
where the time goes in v5:
time: 89.5 us; the launch traced here: 89.3 us
  blocking collectives  73.9 us (83%)
  Pallas kernels  12.2 us (14%)
  starting transfers between devices  1.92 us (2%)
  waiting for transfers between devices  1.13 us (1%)
    all_to_all x1, blocking collectives, on_device(): sums = lax.all_to_all(sums, 'z', 0, 0, tiled=True)  28.8 us
    all_to_all x1, blocking collectives, on_device(): codes = lax.all_to_all(codes, 'w', 0, 0, tiled=True)  16.4 us
    all_to_all x1, blocking collectives, on_device(): sums = lax.all_to_all(sums, 'y', 0, 0, tiled=True)  15.1 us
    all_to_all x1, blocking collectives, on_device(): grads = lax.all_to_all(grads, 'w', 0, 0, tiled=True)  13.6 us
    pallas_call x1, Pallas kernels, on_device(): pl.pallas_call(functools.partial(logits_kernel, sizes), in_specs=[hbm] *...  7.64 us
    ppermute x1, starting transfers between devices, swap(): return lax.ppermute(x, 'c', [(0, 1), (1, 0)])  1.92 us
  transfers between devices with their start and end apart: 1, of which 1 were waited for; matrix products, arithmetic and copies ran while one was open for 0% of the time, Pallas kernels for 1%

profile of v5, /device:TPU:32, one launch (start us, length us, event | category | flops | bytes accessed | tf_op | source)
XLA Modules:
  0.0 89.3 jit_solution(2611611369849994087)
XLA Ops:
  0.0 7.6 %logits.1 = (s16[4,272,512]{2,1,0:T(8,128)(2,1)S(1)}, f32[256,128]{1,0:T(8,128)S(1)}, f32[2,128]{1,0:T(2,128)S(1)}, bf16[256,1152]{1,0:T(8,128)(2,1)S(1)}, bf16[2048,1152]{1,0:T(8,128)(2,1)S(1)}) custom-call(bf16[256,1152]{1,0:T(8,128)(2,1)} %hidden_hbm.1, bf16[2048,1152]{1,0:T(8,128)(2,1)} %weight_hbm.3, s32[1,256]{1,0:T(1,128)} %bitcast.2, f32[1,256]{1,0:T(1,128)} %bitcast.3), custom_call_target="tpu_custom_call" | custom-call | tf_op jit(solution)/shard_map/logits/pallas_call | solution.py:333
  7.6 16.4 %all_to_all.20.codes_ref = s16[4,272,512]{2,1,0:T(8,128)(2,1)S(1)} all-to-all(s16[4,272,512]{2,1,0:T(8,128)(2,1)S(1)} %get-tuple-element.13), channel_id=1, replica_groups=mesh['y'=4,'z'=16,'c'=2,'w'=4] {'w'}, dimensions={0} | all-to-all | bytes 2228224 | tf_op jit(solution)/shard_map/all_to_all | solution.py:359
  24.0 0.7 exponentials.1
  24.7 13.6 %all_to_all.21.grads_ref = bf16[4,272,512]{2,1,0:T(8,128)(2,1)S(1)} all-to-all(bf16[4,272,512]{2,1,0:T(8,128)(2,1)S(1)} %exponentials.1), channel_id=1, replica_groups=mesh['y'=4,'z'=16,'c'=2,'w'=4] {'w'}, dimensions={0} | all-to-all | bytes 2228224 | tf_op jit(solution)/shard_map/all_to_all | solution.py:366
  38.3 1.3 %other_hidden.1 = (s16[1,128,2432]{2,1,0:T(8,128)(2,1)S(1)}, bf16[256,1152]{1,0:T(8,128)(2,1)S(1)}, bf16[2048,1152]{1,0:T(8,128)(2,1)S(1)}) custom-call(bf16[4,272,512]{2,1,0:T(8,128)(2,1)S(1)} %all_to_all.21.grads_ref, bf16[2048,1152]{1,0:T(8,128)(2,1)} %weight_hbm.3, f32[256,128]{1,0:T(8,128)S(1)} %get-tuple-element.14.place_ref, ...), custom_call_target="tpu_custom_call" | custom-call | tf_op jit(solution)/shard_map/other_hidden/pallas_call | solution.py:367
  39.6 1.9 %collective-permute-start = (s16[1,128,2432]{2,1,0:T(8,128)(2,1)S(1)}, s16[1,128,2432]{2,1,0:T(8,128)(2,1)S(1)}, u32[]{:S(2)}, u32[]{:S(2)}) collective-permute-start(s16[1,128,2432]{2,1,0:T(8,128)(2,1)S(1)} %get-tuple-element.19), channel_id=1, source_target_pairs={{0,4},{4,0},{1,5},{5,1},{2,6},{6,2},{3,7},{7,3},{8,12},{12,8},{9,1... | collective-permute-start | bytes 1867784 | tf_op jit(solution)/shard_map/ppermute | solution.py:328
  41.6 0.9 own_hidden.1.mine_ref
  42.4 1.1 %collective-permute-done.other_ref = s16[1,128,2432]{2,1,0:T(8,128)(2,1)S(1)} collective-permute-done((s16[1,128,2432]{2,1,0:T(8,128)(2,1)S(1)}, s16[1,128,2432]{2,1,0:T(8,128)(2,1)S(1)}, u32[]{:S(2)}, u32[]{:S(2)}) %collective-permute-start) | collective-permute-done | bytes 622624 | tf_op jit(solution)/shard_map/ppermute | solution.py:328
  43.6 0.6 sum_cores.1
  44.1 15.1 %all_to_all.22.in_ref = s16[4,32,2432]{2,1,0:T(8,128)(2,1)S(1)} all-to-all(s16[4,32,2432]{2,1,0:T(8,128)(2,1)S(1)} %sum_cores.1), channel_id=1, replica_groups=mesh['y'=4,'z'=16,'c'=2,'w'=4] {'y'}, dimensions={0} | all-to-all | bytes 1245184 | tf_op jit(solution)/shard_map/all_to_all | solution.py:389
  59.2 0.3 sum_y.1
  59.6 28.8 %all_to_all.23 = s16[16,2,2432]{2,1,0:T(2,128)(2,1)S(1)} all-to-all(s16[16,2,2432]{2,1,0:T(2,128)(2,1)S(1)} %sum_y.1), channel_id=1, replica_groups=mesh['y'=4,'z'=16,'c'=2,'w'=4] {'z'}, dimensions={0} | all-to-all | bytes 311296 | tf_op jit(solution)/shard_map/all_to_all | solution.py:396
  88.4 0.1 reshape.11.in_ref
  88.4 0.8 sum_z.1
Async XLA Ops:
  39.6 3.9 %collective-permute-start = (s16[1,128,2432]{2,1,0:T(8,128)(2,1)S(1)}, s16[1,128,2432]{2,1,0:T(8,128)(2,1)S(1)}, u32[]{:S(2)}, u32[]{:S(2)}) collective-permute-start(s16[1,128,2432]{2,1,0:T(8,128)(2,1)S(1)} %get-tuple-element.19), channel_id=1, source_target_pairs={{0,4},{4,0},{1,5},{5,1},{2,6},{6,2},{3,7},{7,3},{8,12},{12,8},{9,1... | collective-permute-start | bytes 1867784 | tf_op jit(solution)/shard_map/ppermute | solution.py:328
